TPU v7x, 512 devices: a whole 4x8x8 slice. The times are simulated.
512 devices in a mesh: gz: 8 (over y), gx: 32 (over x, z), gy: 2 (over core).
Axes of the slice: x: 4, y: 8, z: 8, core: 2. Of those that a mesh axis runs over, the one named last changes fastest.
Arguments:
- electron_density: float32 [128, 512, 512], P('gz', 'gx', 'gy'), may hold values from 0.1 to 4
- hole_density: float32 [128, 512, 512], P('gz', 'gx', 'gy'), may hold values from 0.1 to 4
- potential: float32 [128, 512, 512], P('gz', 'gx', 'gy'), may hold values from -6 to 6
- doping: float32 [128, 512, 512], P('gz', 'gx', 'gy'), may hold values from -6 to 6
- electron_mobility: float32 [128, 512, 512], P('gz', 'gx', 'gy'), may hold values from 0.02 to 0.16
- hole_mobility: float32 [128, 512, 512], P('gz', 'gx', 'gy'), may hold values from 0.02 to 0.16
- cfl_map: int32 [512, 512], P('gx', 'gy'), may hold values from 0 to 8
- fraction: float32 [512, 512], P('gx', 'gy'), may hold values from 0 to 1
Outputs:
- negative_concentration_next: float32 [128, 512, 512], P('gz', 'gx', 'gy')
- positive_concentration_next: float32 [128, 512, 512], P('gz', 'gx', 'gy')
- potential_field: float32 [128, 512, 512], P('gz', 'gx', 'gy')
All inputs are finite; a program needn't handle non-finite values.
Results may differ from a plain program's by a relative error of at most 0.00002.
Values sent between devices are 32-bit elements; how exact they have to be, the bound alone decides.
A program may use at most 128 MiB of HBM per device.

v0:
```python
import jax
import jax.numpy as jnp
from jax import lax
from jax.sharding import PartitionSpec as P

CFL_MAX = 8
DIFFUSION_SWEEPS = 2
JACOBI_SWEEPS = 4


def padded(shard, sides, width):
    for axis, dim in sides:
        devices, length = (lax.axis_size(axis), shard.shape[dim])
        up = [(i, (i + 1) % devices) for i in range(devices - 1)]
        down = [(j, i) for i, j in up]
        last = lax.slice_in_dim(shard, length - width, length, axis=dim)
        first = lax.slice_in_dim(shard, 0, width, axis=dim)
        before = lax.ppermute(last, axis, up)
        after = lax.ppermute(first, axis, down)
        shard = jnp.concatenate([before, shard, after], axis=dim)
    return shard


def neighbours(enlarged_mesh):
    return [
        enlarged_mesh[..., 2:, 1:-1, 1:-1],
        enlarged_mesh[..., :-2, 1:-1, 1:-1],
        enlarged_mesh[..., 1:-1, 2:, 1:-1],
        enlarged_mesh[..., 1:-1, :-2, 1:-1],
        enlarged_mesh[..., 1:-1, 1:-1, 2:],
        enlarged_mesh[..., 1:-1, 1:-1, :-2],
    ]


def upstream(enlarged_mesh, anchor, orient, cfl_map, fraction, layers):
    summed = jnp.zeros((layers,) + cfl_map.shape, jnp.float32)
    for reach_k in range(CFL_MAX + 2):
        weights = jnp.where(cfl_map == reach_k, 1.0 - fraction, 0.0) + jnp.where(
            cfl_map + 1 == reach_k, fraction, 0.0
        )
        offset = anchor + orient * reach_k
        summed = summed + weights[None] * enlarged_mesh[offset : offset + layers]
    return summed


def spread_by_gradient(enlarged_mesh, particle_kinds, linking_factors):
    nearby_sites_list = neighbours(enlarged_mesh)
    concentration_change = linking_factors[0] * (nearby_sites_list[0] - particle_kinds)
    for junction_position in range(1, 6):
        concentration_change = concentration_change + linking_factors[junction_position] * (
            nearby_sites_list[junction_position] - particle_kinds
        )
    return particle_kinds + concentration_change


def relax(enlarged_mesh, charge):
    nearby_sites_list = neighbours(enlarged_mesh)
    summed = (
        nearby_sites_list[0]
        + nearby_sites_list[1]
        + nearby_sites_list[2]
        + nearby_sites_list[3]
        + nearby_sites_list[4]
        + nearby_sites_list[5]
    )
    return (summed + charge) / 6.0


def on_device(
    electron_density,
    hole_density,
    potential,
    doping,
    electron_mobility,
    hole_mobility,
    cfl_map,
    fraction,
):
    layers, rows_x, rows_y = electron_density.shape
    margin = CFL_MAX + 1
    both = jnp.stack([electron_density, hole_density])
    enlarged_mesh = padded(both, (("gz", 1),), margin)
    transported_negative_charges = upstream(enlarged_mesh[0], margin, -1, cfl_map, fraction, layers)
    transported_positive_charges = upstream(enlarged_mesh[1], margin, 1, cfl_map, fraction, layers)
    mobility = padded(
        jnp.stack([electron_mobility, hole_mobility]), (("gz", 1), ("gx", 2), ("gy", 3)), 1
    )
    middle = mobility[:, 1:-1, 1:-1, 1:-1]
    linking_factors = [
        jnp.sqrt(middle * nearby_sites_list) for nearby_sites_list in neighbours(mobility)
    ]
    particle_kinds = jnp.stack([transported_negative_charges, transported_positive_charges])
    for sweep_index in range(DIFFUSION_SWEEPS):
        enlarged_mesh = padded(particle_kinds, (("gz", 1), ("gx", 2), ("gy", 3)), 1)
        particle_kinds = spread_by_gradient(enlarged_mesh, particle_kinds, linking_factors)
    negative_concentration_next = particle_kinds[0]
    positive_concentration_next = particle_kinds[1]
    charge = 0.5 * (positive_concentration_next - negative_concentration_next + doping)
    potential_field = potential
    for sweep_index in range(JACOBI_SWEEPS):
        enlarged_mesh = padded(potential_field, (("gz", 0), ("gx", 1), ("gy", 2)), 1)
        potential_field = relax(enlarged_mesh, charge)
    return (negative_concentration_next, positive_concentration_next, potential_field)


def solution(mesh):
    in_specs = (
        P("gz", "gx", "gy"),
        P("gz", "gx", "gy"),
        P("gz", "gx", "gy"),
        P("gz", "gx", "gy"),
        P("gz", "gx", "gy"),
        P("gz", "gx", "gy"),
        P("gx", "gy"),
        P("gx", "gy"),
    )
    out_specs = (P("gz", "gx", "gy"), P("gz", "gx", "gy"), P("gz", "gx", "gy"))
    return jax.shard_map(
        on_device, mesh=mesh, in_specs=in_specs, out_specs=out_specs, check_vma=False
    )
```

profile of v0, /device:TPU:51, one launch (start us, length us, event | category | flops | bytes accessed | tf_op | source)
XLA Modules:
  0.0 187.8 jit_solution(13924623659405277236)
XLA Ops:
  4.2 3.0 %collective-permute-start.1 = (f32[2,9,16,256]{3,2,1,0:T(8,128)S(1)}, f32[2,9,16,256]{3,2,1,0:T(8,128)S(1)}, u32[]{:S(2)}, u32[]{:S(2)}) collective-permute-start(f32[2,9,16,256]{3,2,1,0:T(8,128)S(1)} %get-tuple-element.27), channel_id=1, source_target_pairs={{64,0},{128,64},{192,128},{256,192},{320,256},{384,320},{448,384},... | collective-permute-start | bytes 884744 | tf_op jit(solution)/shard_map/ppermute | solution.py:19
  7.2 3.1 %collective-permute-start.2 = (f32[2,1,16,256]{3,2,1,0:T(8,128)S(1)}, f32[2,1,16,256]{3,2,1,0:T(8,128)S(1)}, u32[]{:S(2)}, u32[]{:S(2)}) collective-permute-start(f32[2,1,16,256]{3,2,1,0:T(8,128)S(1)} %get-tuple-element.22), channel_id=1, source_target_pairs={{64,0},{128,64},{192,128},{256,192},{320,256},{384,320},{448,384},... | collective-permute-start | bytes 98312 | tf_op jit(solution)/shard_map/ppermute | solution.py:19
  14.7 3.2 %collective-permute-done.21 = f32[1,16,256]{2,1,0:T(8,128)S(1)} collective-permute-done((f32[1,16,256]{2,1,0:T(8,128)S(1)}, f32[1,16,256]{2,1,0:T(8,128)S(1)}, u32[]{:S(2)}, u32[]{:S(2)}) %collective-permute-start.21) | collective-permute-done | bytes 16416 | tf_op jit(solution)/shard_map/ppermute | solution.py:18
  17.9 3.5 %collective-permute-start.20 = (f32[1,16,256]{2,1,0:T(8,128)S(1)}, f32[1,16,256]{2,1,0:T(8,128)S(1)}, u32[]{:S(2)}, u32[]{:S(2)}) collective-permute-start(f32[1,16,256]{2,1,0:T(8,128)S(1)} %get-tuple-element.51), channel_id=1, source_target_pairs={{64,0},{128,64},{192,128},{256,192},{320,256},{384,320},{448,384},... | collective-permute-start | bytes 49160 | tf_op jit(solution)/shard_map/ppermute | solution.py:19
  21.6 10.8 %collective-permute-start.6 = (f32[2,18,1,256]{3,2,1,0:T(1,128)S(1)}, f32[2,18,1,256]{3,2,1,0:T(1,128)S(1)}, u32[]{:S(2)}, u32[]{:S(2)}) collective-permute-start(f32[2,18,1,256]{3,2,1,0:T(1,128)S(1)} %get-tuple-element.16), channel_id=1, source_target_pairs={{2,0},{4,2},{6,4},{8,6},{10,8},{12,10},{14,12},{16,14},{18,16},{20... | collective-permute-start | bytes 110600 | tf_op jit(solution)/shard_map/ppermute | solution.py:19
  34.9 4.1 %collective-permute-start.3 = (f32[2,1,16,256]{3,2,1,0:T(8,128)S(1)}, f32[2,1,16,256]{3,2,1,0:T(8,128)S(1)}, u32[]{:S(2)}, u32[]{:S(2)}) collective-permute-start(f32[2,1,16,256]{3,2,1,0:T(8,128)S(1)} %get-tuple-element.24), channel_id=1, source_target_pairs={{64,0},{128,64},{192,128},{256,192},{320,256},{384,320},{448,384},... | collective-permute-start | bytes 98312 | tf_op jit(solution)/shard_map/ppermute | solution.py:19
  41.1 2.6 %collective-permute-done.5 = f32[2,1,16,256]{3,2,1,0:T(8,128)S(1)} collective-permute-done((f32[2,1,16,256]{3,2,1,0:T(8,128)S(1)}, f32[2,1,16,256]{3,2,1,0:T(8,128)S(1)}, u32[]{:S(2)}, u32[]{:S(2)}) %collective-permute-start.5) | collective-permute-done | bytes 32800 | tf_op jit(solution)/shard_map/ppermute | solution.py:18
  43.8 5.5 %collective-permute-start.7 = (f32[2,18,1,256]{3,2,1,0:T(1,128)S(1)}, f32[2,18,1,256]{3,2,1,0:T(1,128)S(1)}, u32[]{:S(2)}, u32[]{:S(2)}) collective-permute-start(f32[2,18,1,256]{3,2,1,0:T(1,128)S(1)} %get-tuple-element.18), channel_id=1, source_target_pairs={{2,0},{4,2},{6,4},{8,6},{10,8},{12,10},{14,12},{16,14},{18,16},{20... | collective-permute-start | bytes 110600 | tf_op jit(solution)/shard_map/ppermute | solution.py:19
  51.3 7.4 %collective-permute-start.10 = (f32[2,18,18,1]{3,2,1,0:T(8,128)S(1)}, f32[2,18,18,1]{3,2,1,0:T(8,128)S(1)}, u32[]{:S(2)}, u32[]{:S(2)}) collective-permute-start(f32[2,18,18,1]{3,2,1,0:T(8,128)S(1)} %get-tuple-element.10), channel_id=1, source_target_pairs={{1,0},{3,2},{5,4},{7,6},{9,8},{11,10},{13,12},{15,14},{17,16},{19,... | collective-permute-start | bytes 7784 | tf_op jit(solution)/shard_map/ppermute | solution.py:19
  60.4 4.5 %collective-permute-start.11 = (f32[2,18,18,1]{3,2,1,0:T(8,128)S(1)}, f32[2,18,18,1]{3,2,1,0:T(8,128)S(1)}, u32[]{:S(2)}, u32[]{:S(2)}) collective-permute-start(f32[2,18,18,1]{3,2,1,0:T(8,128)S(1)} %get-tuple-element.11), channel_id=1, source_target_pairs={{1,0},{3,2},{5,4},{7,6},{9,8},{11,10},{13,12},{15,14},{17,16},{19,... | collective-permute-start | bytes 7784 | tf_op jit(solution)/shard_map/ppermute | solution.py:19
  68.6 4.0 %fusion.21 = f32[2,16,16,256]{3,2,1,0:T(8,128)S(1)} fusion(f32[2,18,18,1]{3,2,1,0:T(8,128)S(1)} %collective-permute-done.13, f32[2,18,1,256]{3,2,1,0:T(1,128)S(1)} %collective-permute-done.7, f32[2,18,1,256]{3,2,1,0:T(1,128)S(1)} %collective-permute-done.9, f32[2,1,16,256]{3,2,1,0:T(8,128)S(1)} %collective-permute-done.3, ...), kind=kLoop, calls=%fused_computation.55 | loop fusion | flops 9699328 | bytes 1861760 | tf_op jit(solution)/shard_map/add | solution.py:53
  74.6 3.4 %collective-permute-start.15 = (f32[2,1,16,256]{3,2,1,0:T(8,128)S(1)}, f32[2,1,16,256]{3,2,1,0:T(8,128)S(1)}, u32[]{:S(2)}, u32[]{:S(2)}) collective-permute-start(f32[2,1,16,256]{3,2,1,0:T(8,128)S(1)} %get-tuple-element.19), channel_id=1, source_target_pairs={{0,64},{64,128},{128,192},{192,256},{256,320},{320,384},{384,448},... | collective-permute-start | bytes 98312 | tf_op jit(solution)/shard_map/ppermute | solution.py:18
  78.0 4.3 %collective-permute-start.22 = (f32[18,1,256]{2,1,0:T(1,128)S(1)}, f32[18,1,256]{2,1,0:T(1,128)S(1)}, u32[]{:S(2)}, u32[]{:S(2)}) collective-permute-start(f32[18,1,256]{2,1,0:T(1,128)S(1)} %get-tuple-element.44), channel_id=1, source_target_pairs={{2,0},{4,2},{6,4},{8,6},{10,8},{12,10},{14,12},{16,14},{18,16},{20... | collective-permute-start | bytes 55304 | tf_op jit(solution)/shard_map/ppermute | solution.py:19
  84.3 5.5 %collective-permute-start.16 = (f32[2,18,1,256]{3,2,1,0:T(1,128)S(1)}, f32[2,18,1,256]{3,2,1,0:T(1,128)S(1)}, u32[]{:S(2)}, u32[]{:S(2)}) collective-permute-start(f32[2,18,1,256]{3,2,1,0:T(1,128)S(1)} %get-tuple-element.14), channel_id=1, source_target_pairs={{2,0},{4,2},{6,4},{8,6},{10,8},{12,10},{14,12},{16,14},{18,16},{20... | collective-permute-start | bytes 110600 | tf_op jit(solution)/shard_map/ppermute | solution.py:19
  91.8 4.8 %collective-permute-done.17 = f32[2,18,1,256]{3,2,1,0:T(1,128)S(1)} collective-permute-done((f32[2,18,1,256]{3,2,1,0:T(1,128)S(1)}, f32[2,18,1,256]{3,2,1,0:T(1,128)S(1)}, u32[]{:S(2)}, u32[]{:S(2)}) %collective-permute-start.17) | collective-permute-done | bytes 36896 | tf_op jit(solution)/shard_map/ppermute | solution.py:18
  96.9 4.6 %collective-permute-start.18 = (f32[2,18,18,1]{3,2,1,0:T(8,128)S(1)}, f32[2,18,18,1]{3,2,1,0:T(8,128)S(1)}, u32[]{:S(2)}, u32[]{:S(2)}) collective-permute-start(f32[2,18,18,1]{3,2,1,0:T(8,128)S(1)} %get-tuple-element.7), channel_id=1, source_target_pairs={{1,0},{3,2},{5,4},{7,6},{9,8},{11,10},{13,12},{15,14},{17,16},{19,... | collective-permute-start | bytes 7784 | tf_op jit(solution)/shard_map/ppermute | solution.py:19
  103.0 3.1 %collective-permute-start.24 = (f32[18,18,1]{2,1,0:T(8,128)S(1)}, f32[18,18,1]{2,1,0:T(8,128)S(1)}, u32[]{:S(2)}, u32[]{:S(2)}) collective-permute-start(f32[18,18,1]{2,1,0:T(8,128)S(1)} %get-tuple-element.35), channel_id=1, source_target_pairs={{1,0},{3,2},{5,4},{7,6},{9,8},{11,10},{13,12},{15,14},{17,16},{19,... | collective-permute-start | bytes 3896 | tf_op jit(solution)/shard_map/ppermute | solution.py:19
  107.5 4.0 %fusion.3 = f32[2,16,16,256]{3,2,1,0:T(8,128)S(1)} fusion(f32[2,16,16,256]{3,2,1,0:T(8,128)S(1)} %fusion.21, f32[2,18,18,1]{3,2,1,0:T(8,128)S(1)} %collective-permute-done.19, f32[2,18,1,256]{3,2,1,0:T(1,128)S(1)} %collective-permute-done.16, f32[2,18,1,256]{3,2,1,0:T(1,128)S(1)} %collective-permute-done.17, ...), kind=kLoop, calls=%fused_computation.19 | loop fusion | flops 8781824 | bytes 1861760 | tf_op jit(solution)/shard_map/add | solution.py:53
  114.6 3.4 %collective-permute-start.27 = (f32[1,16,256]{2,1,0:T(8,128)S(1)}, f32[1,16,256]{2,1,0:T(8,128)S(1)}, u32[]{:S(2)}, u32[]{:S(2)}) collective-permute-start(f32[1,16,256]{2,1,0:T(8,128)S(1)} %get-tuple-element.49), channel_id=1, source_target_pairs={{0,64},{64,128},{128,192},{192,256},{256,320},{320,384},{384,448},... | collective-permute-start | bytes 49160 | tf_op jit(solution)/shard_map/ppermute | solution.py:18
  121.0 3.4 %collective-permute-start.29 = (f32[18,1,256]{2,1,0:T(1,128)S(1)}, f32[18,1,256]{2,1,0:T(1,128)S(1)}, u32[]{:S(2)}, u32[]{:S(2)}) collective-permute-start(f32[18,1,256]{2,1,0:T(1,128)S(1)} %get-tuple-element.41), channel_id=1, source_target_pairs={{0,2},{2,4},{4,6},{6,8},{8,10},{10,12},{12,14},{14,16},{16,18},{18... | collective-permute-start | bytes 55304 | tf_op jit(solution)/shard_map/ppermute | solution.py:18
  124.4 3.2 %collective-permute-done.29 = f32[18,1,256]{2,1,0:T(1,128)S(1)} collective-permute-done((f32[18,1,256]{2,1,0:T(1,128)S(1)}, f32[18,1,256]{2,1,0:T(1,128)S(1)}, u32[]{:S(2)}, u32[]{:S(2)}) %collective-permute-start.29) | collective-permute-done | bytes 18464 | tf_op jit(solution)/shard_map/ppermute | solution.py:18
  127.8 5.4 %collective-permute-start.30 = (f32[18,18,1]{2,1,0:T(8,128)S(1)}, f32[18,18,1]{2,1,0:T(8,128)S(1)}, u32[]{:S(2)}, u32[]{:S(2)}) collective-permute-start(f32[18,18,1]{2,1,0:T(8,128)S(1)} %get-tuple-element.33), channel_id=1, source_target_pairs={{1,0},{3,2},{5,4},{7,6},{9,8},{11,10},{13,12},{15,14},{17,16},{19,... | collective-permute-start | bytes 3896 | tf_op jit(solution)/shard_map/ppermute | solution.py:19
  136.9 2.8 %collective-permute-start.32 = (f32[1,16,256]{2,1,0:T(8,128)S(1)}, f32[1,16,256]{2,1,0:T(8,128)S(1)}, u32[]{:S(2)}, u32[]{:S(2)}) collective-permute-start(f32[1,16,256]{2,1,0:T(8,128)S(1)} %get-tuple-element.48), channel_id=1, source_target_pairs={{64,0},{128,64},{192,128},{256,192},{320,256},{384,320},{448,384},... | collective-permute-start | bytes 49160 | tf_op jit(solution)/shard_map/ppermute | solution.py:19
  142.2 2.7 %collective-permute-done.33 = f32[1,16,256]{2,1,0:T(8,128)S(1)} collective-permute-done((f32[1,16,256]{2,1,0:T(8,128)S(1)}, f32[1,16,256]{2,1,0:T(8,128)S(1)}, u32[]{:S(2)}, u32[]{:S(2)}) %collective-permute-start.33) | collective-permute-done | bytes 16416 | tf_op jit(solution)/shard_map/ppermute | solution.py:18
  146.9 3.4 %collective-permute-start.35 = (f32[18,1,256]{2,1,0:T(1,128)S(1)}, f32[18,1,256]{2,1,0:T(1,128)S(1)}, u32[]{:S(2)}, u32[]{:S(2)}) collective-permute-start(f32[18,1,256]{2,1,0:T(1,128)S(1)} %get-tuple-element.39), channel_id=1, source_target_pairs={{0,2},{2,4},{4,6},{6,8},{8,10},{10,12},{12,14},{14,16},{16,18},{18... | collective-permute-start | bytes 55304 | tf_op jit(solution)/shard_map/ppermute | solution.py:18
  150.3 3.2 %collective-permute-done.35 = f32[18,1,256]{2,1,0:T(1,128)S(1)} collective-permute-done((f32[18,1,256]{2,1,0:T(1,128)S(1)}, f32[18,1,256]{2,1,0:T(1,128)S(1)}, u32[]{:S(2)}, u32[]{:S(2)}) %collective-permute-start.35) | collective-permute-done | bytes 18464 | tf_op jit(solution)/shard_map/ppermute | solution.py:18
  153.7 4.4 %collective-permute-start.36 = (f32[18,18,1]{2,1,0:T(8,128)S(1)}, f32[18,18,1]{2,1,0:T(8,128)S(1)}, u32[]{:S(2)}, u32[]{:S(2)}) collective-permute-start(f32[18,18,1]{2,1,0:T(8,128)S(1)} %get-tuple-element.31), channel_id=1, source_target_pairs={{1,0},{3,2},{5,4},{7,6},{9,8},{11,10},{13,12},{15,14},{17,16},{19,... | collective-permute-start | bytes 3896 | tf_op jit(solution)/shard_map/ppermute | solution.py:19
  161.8 3.6 %collective-permute-start.38 = (f32[1,16,256]{2,1,0:T(8,128)S(1)}, f32[1,16,256]{2,1,0:T(8,128)S(1)}, u32[]{:S(2)}, u32[]{:S(2)}) collective-permute-start(f32[1,16,256]{2,1,0:T(8,128)S(1)} %get-tuple-element.46), channel_id=1, source_target_pairs={{64,0},{128,64},{192,128},{256,192},{320,256},{384,320},{448,384},... | collective-permute-start | bytes 49160 | tf_op jit(solution)/shard_map/ppermute | solution.py:19
  167.4 2.5 %collective-permute-done.39 = f32[1,16,256]{2,1,0:T(8,128)S(1)} collective-permute-done((f32[1,16,256]{2,1,0:T(8,128)S(1)}, f32[1,16,256]{2,1,0:T(8,128)S(1)}, u32[]{:S(2)}, u32[]{:S(2)}) %collective-permute-start.39) | collective-permute-done | bytes 16416 | tf_op jit(solution)/shard_map/ppermute | solution.py:18
  171.9 3.4 %collective-permute-start.41 = (f32[18,1,256]{2,1,0:T(1,128)S(1)}, f32[18,1,256]{2,1,0:T(1,128)S(1)}, u32[]{:S(2)}, u32[]{:S(2)}) collective-permute-start(f32[18,1,256]{2,1,0:T(1,128)S(1)} %get-tuple-element.37), channel_id=1, source_target_pairs={{0,2},{2,4},{4,6},{6,8},{8,10},{10,12},{12,14},{14,16},{16,18},{18... | collective-permute-start | bytes 55304 | tf_op jit(solution)/shard_map/ppermute | solution.py:18
  175.3 3.2 %collective-permute-done.41 = f32[18,1,256]{2,1,0:T(1,128)S(1)} collective-permute-done((f32[18,1,256]{2,1,0:T(1,128)S(1)}, f32[18,1,256]{2,1,0:T(1,128)S(1)}, u32[]{:S(2)}, u32[]{:S(2)}) %collective-permute-start.41) | collective-permute-done | bytes 18464 | tf_op jit(solution)/shard_map/ppermute | solution.py:18
  178.7 4.6 %collective-permute-start.42 = (f32[18,18,1]{2,1,0:T(8,128)S(1)}, f32[18,18,1]{2,1,0:T(8,128)S(1)}, u32[]{:S(2)}, u32[]{:S(2)}) collective-permute-start(f32[18,18,1]{2,1,0:T(8,128)S(1)} %get-tuple-element.29), channel_id=1, source_target_pairs={{1,0},{3,2},{5,4},{7,6},{9,8},{11,10},{13,12},{15,14},{17,16},{19,... | collective-permute-start | bytes 3896 | tf_op jit(solution)/shard_map/ppermute | solution.py:19
  (114 shorter events, 55.6 us)
Async XLA Ops:
  1.9 32.4 %collective-permute-start = (f32[2,9,16,256]{3,2,1,0:T(8,128)S(1)}, f32[2,9,16,256]{3,2,1,0:T(8,128)S(1)}, u32[]{:S(2)}, u32[]{:S(2)}) collective-permute-start(f32[2,9,16,256]{3,2,1,0:T(8,128)S(1)} %get-tuple-element.28), channel_id=1, source_target_pairs={{0,64},{64,128},{128,192},{192,256},{256,320},{320,384},{384,448},... | collective-permute-start | bytes 884744 | tf_op jit(solution)/shard_map/ppermute | solution.py:18
  4.2 30.1 %collective-permute-start.1 = (f32[2,9,16,256]{3,2,1,0:T(8,128)S(1)}, f32[2,9,16,256]{3,2,1,0:T(8,128)S(1)}, u32[]{:S(2)}, u32[]{:S(2)}) collective-permute-start(f32[2,9,16,256]{3,2,1,0:T(8,128)S(1)} %get-tuple-element.27), channel_id=1, source_target_pairs={{64,0},{128,64},{192,128},{256,192},{320,256},{384,320},{448,384},... | collective-permute-start | bytes 884744 | tf_op jit(solution)/shard_map/ppermute | solution.py:19
  7.2 14.3 %collective-permute-start.2 = (f32[2,1,16,256]{3,2,1,0:T(8,128)S(1)}, f32[2,1,16,256]{3,2,1,0:T(8,128)S(1)}, u32[]{:S(2)}, u32[]{:S(2)}) collective-permute-start(f32[2,1,16,256]{3,2,1,0:T(8,128)S(1)} %get-tuple-element.22), channel_id=1, source_target_pairs={{64,0},{128,64},{192,128},{256,192},{320,256},{384,320},{448,384},... | collective-permute-start | bytes 98312 | tf_op jit(solution)/shard_map/ppermute | solution.py:19
  10.4 11.1 %collective-permute-start.4 = (f32[2,1,16,256]{3,2,1,0:T(8,128)S(1)}, f32[2,1,16,256]{3,2,1,0:T(8,128)S(1)}, u32[]{:S(2)}, u32[]{:S(2)}) collective-permute-start(f32[2,1,16,256]{3,2,1,0:T(8,128)S(1)} %get-tuple-element.21), channel_id=1, source_target_pairs={{0,64},{64,128},{128,192},{192,256},{256,320},{320,384},{384,448},... | collective-permute-start | bytes 98312 | tf_op jit(solution)/shard_map/ppermute | solution.py:18
  17.9 48.3 %collective-permute-start.20 = (f32[1,16,256]{2,1,0:T(8,128)S(1)}, f32[1,16,256]{2,1,0:T(8,128)S(1)}, u32[]{:S(2)}, u32[]{:S(2)}) collective-permute-start(f32[1,16,256]{2,1,0:T(8,128)S(1)} %get-tuple-element.51), channel_id=1, source_target_pairs={{64,0},{128,64},{192,128},{256,192},{320,256},{384,320},{448,384},... | collective-permute-start | bytes 49160 | tf_op jit(solution)/shard_map/ppermute | solution.py:19
  21.6 19.4 %collective-permute-start.6 = (f32[2,18,1,256]{3,2,1,0:T(1,128)S(1)}, f32[2,18,1,256]{3,2,1,0:T(1,128)S(1)}, u32[]{:S(2)}, u32[]{:S(2)}) collective-permute-start(f32[2,18,1,256]{3,2,1,0:T(1,128)S(1)} %get-tuple-element.16), channel_id=1, source_target_pairs={{2,0},{4,2},{6,4},{8,6},{10,8},{12,10},{14,12},{16,14},{18,16},{20... | collective-permute-start | bytes 110600 | tf_op jit(solution)/shard_map/ppermute | solution.py:19
  32.4 8.6 %collective-permute-start.8 = (f32[2,18,1,256]{3,2,1,0:T(1,128)S(1)}, f32[2,18,1,256]{3,2,1,0:T(1,128)S(1)}, u32[]{:S(2)}, u32[]{:S(2)}) collective-permute-start(f32[2,18,1,256]{3,2,1,0:T(1,128)S(1)} %get-tuple-element.15), channel_id=1, source_target_pairs={{0,2},{2,4},{4,6},{6,8},{8,10},{10,12},{12,14},{14,16},{16,18},{18... | collective-permute-start | bytes 110600 | tf_op jit(solution)/shard_map/ppermute | solution.py:18
  34.9 6.2 %collective-permute-start.3 = (f32[2,1,16,256]{3,2,1,0:T(8,128)S(1)}, f32[2,1,16,256]{3,2,1,0:T(8,128)S(1)}, u32[]{:S(2)}, u32[]{:S(2)}) collective-permute-start(f32[2,1,16,256]{3,2,1,0:T(8,128)S(1)} %get-tuple-element.24), channel_id=1, source_target_pairs={{64,0},{128,64},{192,128},{256,192},{320,256},{384,320},{448,384},... | collective-permute-start | bytes 98312 | tf_op jit(solution)/shard_map/ppermute | solution.py:19
  43.8 16.3 %collective-permute-start.7 = (f32[2,18,1,256]{3,2,1,0:T(1,128)S(1)}, f32[2,18,1,256]{3,2,1,0:T(1,128)S(1)}, u32[]{:S(2)}, u32[]{:S(2)}) collective-permute-start(f32[2,18,1,256]{3,2,1,0:T(1,128)S(1)} %get-tuple-element.18), channel_id=1, source_target_pairs={{2,0},{4,2},{6,4},{8,6},{10,8},{12,10},{14,12},{16,14},{18,16},{20... | collective-permute-start | bytes 110600 | tf_op jit(solution)/shard_map/ppermute | solution.py:19
  49.2 10.9 %collective-permute-start.9 = (f32[2,18,1,256]{3,2,1,0:T(1,128)S(1)}, f32[2,18,1,256]{3,2,1,0:T(1,128)S(1)}, u32[]{:S(2)}, u32[]{:S(2)}) collective-permute-start(f32[2,18,1,256]{3,2,1,0:T(1,128)S(1)} %get-tuple-element.17), channel_id=1, source_target_pairs={{0,2},{2,4},{4,6},{6,8},{8,10},{10,12},{12,14},{14,16},{16,18},{18... | collective-permute-start | bytes 110600 | tf_op jit(solution)/shard_map/ppermute | solution.py:18
  51.3 14.9 %collective-permute-start.10 = (f32[2,18,18,1]{3,2,1,0:T(8,128)S(1)}, f32[2,18,18,1]{3,2,1,0:T(8,128)S(1)}, u32[]{:S(2)}, u32[]{:S(2)}) collective-permute-start(f32[2,18,18,1]{3,2,1,0:T(8,128)S(1)} %get-tuple-element.10), channel_id=1, source_target_pairs={{1,0},{3,2},{5,4},{7,6},{9,8},{11,10},{13,12},{15,14},{17,16},{19,... | collective-permute-start | bytes 7784 | tf_op jit(solution)/shard_map/ppermute | solution.py:19
  58.8 7.5 %collective-permute-start.12 = (f32[2,18,18,1]{3,2,1,0:T(8,128)S(1)}, f32[2,18,18,1]{3,2,1,0:T(8,128)S(1)}, u32[]{:S(2)}, u32[]{:S(2)}) collective-permute-start(f32[2,18,18,1]{3,2,1,0:T(8,128)S(1)} %get-tuple-element.9), channel_id=1, source_target_pairs={{0,1},{2,3},{4,5},{6,7},{8,9},{10,11},{12,13},{14,15},{16,17},{18,... | collective-permute-start | bytes 7784 | tf_op jit(solution)/shard_map/ppermute | solution.py:18
  60.4 5.9 %collective-permute-start.11 = (f32[2,18,18,1]{3,2,1,0:T(8,128)S(1)}, f32[2,18,18,1]{3,2,1,0:T(8,128)S(1)}, u32[]{:S(2)}, u32[]{:S(2)}) collective-permute-start(f32[2,18,18,1]{3,2,1,0:T(8,128)S(1)} %get-tuple-element.11), channel_id=1, source_target_pairs={{1,0},{3,2},{5,4},{7,6},{9,8},{11,10},{13,12},{15,14},{17,16},{19,... | collective-permute-start | bytes 7784 | tf_op jit(solution)/shard_map/ppermute | solution.py:19
  72.7 11.6 %collective-permute-start.14 = (f32[2,1,16,256]{3,2,1,0:T(8,128)S(1)}, f32[2,1,16,256]{3,2,1,0:T(8,128)S(1)}, u32[]{:S(2)}, u32[]{:S(2)}) collective-permute-start(f32[2,1,16,256]{3,2,1,0:T(8,128)S(1)} %get-tuple-element.20), channel_id=1, source_target_pairs={{64,0},{128,64},{192,128},{256,192},{320,256},{384,320},{448,384},... | collective-permute-start | bytes 98312 | tf_op jit(solution)/shard_map/ppermute | solution.py:19
  74.6 9.7 %collective-permute-start.15 = (f32[2,1,16,256]{3,2,1,0:T(8,128)S(1)}, f32[2,1,16,256]{3,2,1,0:T(8,128)S(1)}, u32[]{:S(2)}, u32[]{:S(2)}) collective-permute-start(f32[2,1,16,256]{3,2,1,0:T(8,128)S(1)} %get-tuple-element.19), channel_id=1, source_target_pairs={{0,64},{64,128},{128,192},{192,256},{256,320},{320,384},{384,448},... | collective-permute-start | bytes 98312 | tf_op jit(solution)/shard_map/ppermute | solution.py:18
  78.0 13.7 %collective-permute-start.22 = (f32[18,1,256]{2,1,0:T(1,128)S(1)}, f32[18,1,256]{2,1,0:T(1,128)S(1)}, u32[]{:S(2)}, u32[]{:S(2)}) collective-permute-start(f32[18,1,256]{2,1,0:T(1,128)S(1)} %get-tuple-element.44), channel_id=1, source_target_pairs={{2,0},{4,2},{6,4},{8,6},{10,8},{12,10},{14,12},{16,14},{18,16},{20... | collective-permute-start | bytes 55304 | tf_op jit(solution)/shard_map/ppermute | solution.py:19
  82.3 9.4 %collective-permute-start.23 = (f32[18,1,256]{2,1,0:T(1,128)S(1)}, f32[18,1,256]{2,1,0:T(1,128)S(1)}, u32[]{:S(2)}, u32[]{:S(2)}) collective-permute-start(f32[18,1,256]{2,1,0:T(1,128)S(1)} %get-tuple-element.43), channel_id=1, source_target_pairs={{0,2},{2,4},{4,6},{6,8},{8,10},{10,12},{12,14},{14,16},{16,18},{18... | collective-permute-start | bytes 55304 | tf_op jit(solution)/shard_map/ppermute | solution.py:18
  84.3 7.5 %collective-permute-start.16 = (f32[2,18,1,256]{3,2,1,0:T(1,128)S(1)}, f32[2,18,1,256]{3,2,1,0:T(1,128)S(1)}, u32[]{:S(2)}, u32[]{:S(2)}) collective-permute-start(f32[2,18,1,256]{3,2,1,0:T(1,128)S(1)} %get-tuple-element.14), channel_id=1, source_target_pairs={{2,0},{4,2},{6,4},{8,6},{10,8},{12,10},{14,12},{16,14},{18,16},{20... | collective-permute-start | bytes 110600 | tf_op jit(solution)/shard_map/ppermute | solution.py:19
  89.8 6.8 %collective-permute-start.17 = (f32[2,18,1,256]{3,2,1,0:T(1,128)S(1)}, f32[2,18,1,256]{3,2,1,0:T(1,128)S(1)}, u32[]{:S(2)}, u32[]{:S(2)}) collective-permute-start(f32[2,18,1,256]{3,2,1,0:T(1,128)S(1)} %get-tuple-element.13), channel_id=1, source_target_pairs={{0,2},{2,4},{4,6},{6,8},{8,10},{10,12},{12,14},{14,16},{16,18},{18... | collective-permute-start | bytes 110600 | tf_op jit(solution)/shard_map/ppermute | solution.py:18
  96.9 10.6 %collective-permute-start.18 = (f32[2,18,18,1]{3,2,1,0:T(8,128)S(1)}, f32[2,18,18,1]{3,2,1,0:T(8,128)S(1)}, u32[]{:S(2)}, u32[]{:S(2)}) collective-permute-start(f32[2,18,18,1]{3,2,1,0:T(8,128)S(1)} %get-tuple-element.7), channel_id=1, source_target_pairs={{1,0},{3,2},{5,4},{7,6},{9,8},{11,10},{13,12},{15,14},{17,16},{19,... | collective-permute-start | bytes 7784 | tf_op jit(solution)/shard_map/ppermute | solution.py:19
  101.6 6.0 %collective-permute-start.19 = (f32[2,18,18,1]{3,2,1,0:T(8,128)S(1)}, f32[2,18,18,1]{3,2,1,0:T(8,128)S(1)}, u32[]{:S(2)}, u32[]{:S(2)}) collective-permute-start(f32[2,18,18,1]{3,2,1,0:T(8,128)S(1)} %get-tuple-element.8), channel_id=1, source_target_pairs={{0,1},{2,3},{4,5},{6,7},{8,9},{10,11},{12,13},{14,15},{16,17},{18,... | collective-permute-start | bytes 7784 | tf_op jit(solution)/shard_map/ppermute | solution.py:18
  103.0 8.5 %collective-permute-start.24 = (f32[18,18,1]{2,1,0:T(8,128)S(1)}, f32[18,18,1]{2,1,0:T(8,128)S(1)}, u32[]{:S(2)}, u32[]{:S(2)}) collective-permute-start(f32[18,18,1]{2,1,0:T(8,128)S(1)} %get-tuple-element.35), channel_id=1, source_target_pairs={{1,0},{3,2},{5,4},{7,6},{9,8},{11,10},{13,12},{15,14},{17,16},{19,... | collective-permute-start | bytes 3896 | tf_op jit(solution)/shard_map/ppermute | solution.py:19
  106.1 5.5 %collective-permute-start.25 = (f32[18,18,1]{2,1,0:T(8,128)S(1)}, f32[18,18,1]{2,1,0:T(8,128)S(1)}, u32[]{:S(2)}, u32[]{:S(2)}) collective-permute-start(f32[18,18,1]{2,1,0:T(8,128)S(1)} %get-tuple-element.36), channel_id=1, source_target_pairs={{0,1},{2,3},{4,5},{6,7},{8,9},{10,11},{12,13},{14,15},{16,17},{18,... | collective-permute-start | bytes 3896 | tf_op jit(solution)/shard_map/ppermute | solution.py:18
  119.1 5.3 %collective-permute-start.28 = (f32[18,1,256]{2,1,0:T(1,128)S(1)}, f32[18,1,256]{2,1,0:T(1,128)S(1)}, u32[]{:S(2)}, u32[]{:S(2)}) collective-permute-start(f32[18,1,256]{2,1,0:T(1,128)S(1)} %get-tuple-element.42), channel_id=1, source_target_pairs={{2,0},{4,2},{6,4},{8,6},{10,8},{12,10},{14,12},{16,14},{18,16},{20... | collective-permute-start | bytes 55304 | tf_op jit(solution)/shard_map/ppermute | solution.py:19
  121.0 6.6 %collective-permute-start.29 = (f32[18,1,256]{2,1,0:T(1,128)S(1)}, f32[18,1,256]{2,1,0:T(1,128)S(1)}, u32[]{:S(2)}, u32[]{:S(2)}) collective-permute-start(f32[18,1,256]{2,1,0:T(1,128)S(1)} %get-tuple-element.41), channel_id=1, source_target_pairs={{0,2},{2,4},{4,6},{6,8},{8,10},{10,12},{12,14},{14,16},{16,18},{18... | collective-permute-start | bytes 55304 | tf_op jit(solution)/shard_map/ppermute | solution.py:18
  127.8 6.7 %collective-permute-start.30 = (f32[18,18,1]{2,1,0:T(8,128)S(1)}, f32[18,18,1]{2,1,0:T(8,128)S(1)}, u32[]{:S(2)}, u32[]{:S(2)}) collective-permute-start(f32[18,18,1]{2,1,0:T(8,128)S(1)} %get-tuple-element.33), channel_id=1, source_target_pairs={{1,0},{3,2},{5,4},{7,6},{9,8},{11,10},{13,12},{15,14},{17,16},{19,... | collective-permute-start | bytes 3896 | tf_op jit(solution)/shard_map/ppermute | solution.py:19
  145.0 5.3 %collective-permute-start.34 = (f32[18,1,256]{2,1,0:T(1,128)S(1)}, f32[18,1,256]{2,1,0:T(1,128)S(1)}, u32[]{:S(2)}, u32[]{:S(2)}) collective-permute-start(f32[18,1,256]{2,1,0:T(1,128)S(1)} %get-tuple-element.40), channel_id=1, source_target_pairs={{2,0},{4,2},{6,4},{8,6},{10,8},{12,10},{14,12},{16,14},{18,16},{20... | collective-permute-start | bytes 55304 | tf_op jit(solution)/shard_map/ppermute | solution.py:19
  146.9 6.6 %collective-permute-start.35 = (f32[18,1,256]{2,1,0:T(1,128)S(1)}, f32[18,1,256]{2,1,0:T(1,128)S(1)}, u32[]{:S(2)}, u32[]{:S(2)}) collective-permute-start(f32[18,1,256]{2,1,0:T(1,128)S(1)} %get-tuple-element.39), channel_id=1, source_target_pairs={{0,2},{2,4},{4,6},{6,8},{8,10},{10,12},{12,14},{14,16},{16,18},{18... | collective-permute-start | bytes 55304 | tf_op jit(solution)/shard_map/ppermute | solution.py:18
  153.7 5.7 %collective-permute-start.36 = (f32[18,18,1]{2,1,0:T(8,128)S(1)}, f32[18,18,1]{2,1,0:T(8,128)S(1)}, u32[]{:S(2)}, u32[]{:S(2)}) collective-permute-start(f32[18,18,1]{2,1,0:T(8,128)S(1)} %get-tuple-element.31), channel_id=1, source_target_pairs={{1,0},{3,2},{5,4},{7,6},{9,8},{11,10},{13,12},{15,14},{17,16},{19,... | collective-permute-start | bytes 3896 | tf_op jit(solution)/shard_map/ppermute | solution.py:19
  161.8 5.6 %collective-permute-start.38 = (f32[1,16,256]{2,1,0:T(8,128)S(1)}, f32[1,16,256]{2,1,0:T(8,128)S(1)}, u32[]{:S(2)}, u32[]{:S(2)}) collective-permute-start(f32[1,16,256]{2,1,0:T(8,128)S(1)} %get-tuple-element.46), channel_id=1, source_target_pairs={{64,0},{128,64},{192,128},{256,192},{320,256},{384,320},{448,384},... | collective-permute-start | bytes 49160 | tf_op jit(solution)/shard_map/ppermute | solution.py:19
  171.9 6.6 %collective-permute-start.41 = (f32[18,1,256]{2,1,0:T(1,128)S(1)}, f32[18,1,256]{2,1,0:T(1,128)S(1)}, u32[]{:S(2)}, u32[]{:S(2)}) collective-permute-start(f32[18,1,256]{2,1,0:T(1,128)S(1)} %get-tuple-element.37), channel_id=1, source_target_pairs={{0,2},{2,4},{4,6},{6,8},{8,10},{10,12},{12,14},{14,16},{16,18},{18... | collective-permute-start | bytes 55304 | tf_op jit(solution)/shard_map/ppermute | solution.py:18
  178.7 6.0 %collective-permute-start.42 = (f32[18,18,1]{2,1,0:T(8,128)S(1)}, f32[18,18,1]{2,1,0:T(8,128)S(1)}, u32[]{:S(2)}, u32[]{:S(2)}) collective-permute-start(f32[18,18,1]{2,1,0:T(8,128)S(1)} %get-tuple-element.29), channel_id=1, source_target_pairs={{1,0},{3,2},{5,4},{7,6},{9,8},{11,10},{13,12},{15,14},{17,16},{19,... | collective-permute-start | bytes 3896 | tf_op jit(solution)/shard_map/ppermute | solution.py:19
  (20 other events, 112.0 us)
where the time goes:
time: 189 us; the launch traced here: 188 us
  starting transfers between devices  136 us (72%)
  waiting for transfers between devices  35.3 us (19%)
  other arithmetic  13.5 us (7%)
    ppermute x22, starting transfers between devices, padded(): after = lax.ppermute(first, axis, down)  89.8 us
    ppermute x22, starting transfers between devices, padded(): before = lax.ppermute(last, axis, up)  46.5 us
    ppermute x22, waiting for transfers between devices, padded(): before = lax.ppermute(last, axis, up)  35.2 us
    add x2, other arithmetic, spread_by_gradient(): return particle_kinds + concentration_change  8 us
  transfers between devices with their start and end apart: 44, of which 13 were waited for; matrix products, arithmetic and copies ran while one was open for 3% of the time, Pallas kernels for 0%

commit v1 on v0

v1 whole, which is shorter than its diff:
```python
import jax
import jax.numpy as jnp
from jax import lax
from jax.experimental import pallas as pl
from jax.experimental.pallas import tpu as pltpu
from jax.sharding import PartitionSpec as P

MESH = pl.DeviceIdType.MESH

CFL_MAX = 8
NZ = 16
NR = 16
NL = 256
OWN = 8
OFF = 4
TILES = 4
ROWS = 24
TOP = 4
FIRST = TOP + OFF
SWEEP_HALO = 2
UP = CFL_MAX + 1 + SWEEP_HALO

E, H, ME, MH, PHI, DOP, CFL, FRAC = range(8)
REACH = {
    E: (2, UP, 2),
    H: (2, 2, UP),
    ME: (2, 2, 2),
    MH: (2, 2, 2),
    PHI: (4, 4, 4),
    DOP: (0, 0, 0),
    CFL: (2, 0, 0),
    FRAC: (2, 0, 0),
}
FLAT = (CFL, FRAC)


def received_rows(field):
    rows, below, above = REACH[field]
    if field in FLAT:
        return OWN + 2 * rows
    near = (NZ + below + above) * (OWN + rows)
    if rows == 0:
        return near
    return near + (NZ + below + above - 2) * rows


def sent_rows(field, dz):
    rows, below, above = REACH[field]
    if field in FLAT:
        return (OWN + rows) + 2 * rows if dz == 0 else 0
    if dz == 0:
        return NZ * (OWN + rows) + 2 * NZ * rows
    depth = below if dz == 1 else above
    if depth == 0:
        return 0
    return depth * 2 * (OWN + rows) + 2 * (depth - 1) * rows


def kernel(sizes, *refs):
    n_gz, n_gx = sizes
    ins = refs[:8]
    outs = refs[8:11]
    land = refs[11:19]
    (s_buf, rs_buf, a_buf, q0, q1, c_buf, v_a, v_b, u_a, u_b, stage, count, in_send, in_recv, c_send, c_recv, o_send,
     o_recv) = refs[19:]
    g, w, c = lax.axis_index("gz"), lax.axis_index("gx"), lax.axis_index("gy")

    def at(dz, dx, core):
        return (lax.rem(g + (dz + n_gz), n_gz), lax.rem(w + (dx + n_gx), n_gx), core)

    barrier = pltpu.get_barrier_semaphore()
    side = 2 * c - 1
    for dz in (0, 1, -1):
        if dz != 0:
            pl.semaphore_signal(barrier, inc=1, device_id=at(dz, 0, c), device_id_type=MESH)
        pl.semaphore_signal(barrier, inc=1, device_id=at(dz, 0, 1 - c), device_id_type=MESH)
        for core in (0, 1):
            pl.semaphore_signal(barrier, inc=1, device_id=at(dz, side, core), device_id_type=MESH)
    pl.semaphore_wait(barrier, 11)

    lanes = pl.ds(pl.multiple_of(c * NL, NL), NL)

    def push(field, dz, piece):
        if piece in (0, 1):
            move(field, dz, 0, piece, piece)
        elif piece == "right":
            move(field, dz, 1, 0, piece)
        else:
            move(field, dz, -1, 1, piece)

    def move(field, dz, dx, core, piece):
        rows, below, above = REACH[field]
        clip = abs(dx)
        depth = {0: NZ, 1: below - clip, -1: above - clip}[dz]
        if depth <= 0 or (rows == 0 and clip) or (field in FLAT and dz != 0):
            return
        pieces = {
            0: [(0, 0, OWN), (OWN, OWN, rows)],
            1: [(OWN, 0, OWN), (OWN - rows, NR - rows, rows)],
            "right": [(NR - rows, NR - rows, rows)],
            "left": [(0, OWN, rows)],
        }[piece]
        for src_x, dst_x, size in pieces:
            if size == 0:
                continue
            src_x, dst_x = pl.ds(src_x, size), pl.ds(dst_x, size)
            if field in FLAT:
                src, dst = ins[field].at[src_x, :], land[field].at[dst_x, lanes]
            else:
                src_z, dst_z = {0: (0, below), 1: (NZ - depth, below - depth), -1: (0, below + NZ)}[dz]
                src = ins[field].at[pl.ds(src_z, depth), src_x, :]
                dst = land[field].at[pl.ds(dst_z, depth), dst_x, lanes]
            send(field, dz, dx, core, src, dst)

    def send(field, dz, dx, core, src, dst):
        def remote():
            pltpu.make_async_remote_copy(
                src_ref=src,
                dst_ref=dst,
                send_sem=in_send.at[field, dz + 1],
                recv_sem=in_recv.at[field],
                device_id=at(dz, dx, core),
                device_id_type=MESH,
            ).start()

        if dz == 0 and dx == 0:

            @pl.when(c == core)
            def _():
                pltpu.make_async_copy(src, dst, in_recv.at[field]).start()

            @pl.when(c != core)
            def _():
                remote()
        else:
            remote()

    def arrived(field):
        view = count.at[pl.ds(0, TILES * received_rows(field)), :]
        pltpu.make_async_copy(view, view, in_recv.at[field]).wait()

    for field in (ME, MH):
        for dz in (1, -1):
            for piece in ("right", "left", 0, 1):
                push(field, dz, piece)
    for field, dz in ((E, 1), (H, -1)):
        for piece in ("right", "left"):
            push(field, dz, piece)
    for field, dz in ((E, 1), (H, -1)):
        for piece in (0, 1):
            push(field, dz, piece)
    for field in (ME, MH):
        for piece in ("right", "left", 0, 1):
            push(field, 0, piece)
    for field, dz in ((E, -1), (H, 1)):
        for piece in ("right", "left", 0, 1):
            push(field, dz, piece)
    for field in (E, H, CFL, FRAC):
        for piece in ("right", "left", 0, 1):
            push(field, 0, piece)
    for dz in (1, -1, 0):
        for piece in ("right", "left", 0, 1):
            push(PHI, dz, piece)
    for piece in (0, 1):
        push(DOP, 0, piece)

    row = lax.broadcasted_iota(jnp.int32, (NR, 128), 0)
    out_left = jnp.logical_and(w == 0, c == 0)
    out_right = jnp.logical_and(w == n_gx - 1, c == 1)
    first_row = jnp.where(out_left, OFF, 0)
    last_row = jnp.where(out_right, OFF + OWN, NR)
    inside = jnp.where(jnp.logical_and(row >= first_row, row < last_row), 1.0, 0.0)
    halo_row = lax.broadcasted_iota(jnp.int32, (8, 128), 0)
    halo_out = jnp.where(halo_row < OFF, jnp.where(out_right, 1, 0), jnp.where(out_left, 1, 0))
    halo_inside = jnp.where(halo_out == 0, 1.0, 0.0)
    lane = lax.broadcasted_iota(jnp.int32, (NR, 128), 1)
    at_first, at_last = lane == 0, lane == 127
    lo_end, hi_end = g == 0, g == n_gz - 1

    def layer_in(z, below):
        first = jnp.where(lo_end, below, 0)
        last = jnp.where(hi_end, below + NZ, below + NZ + below)
        return jnp.where(jnp.logical_and(z >= first, z < last), 1.0, 0.0)

    def around(ref, z, start, rows):
        centre = [ref[z, t, pl.ds(start, rows), :] for t in range(TILES)]
        up = [pltpu.roll(v, 127, 1) for v in centre] + [jnp.zeros((rows, 128), jnp.float32)]
        down = [jnp.zeros((rows, 128), jnp.float32)] + [pltpu.roll(v, 1, 1) for v in centre]
        is_first, is_last = at_first[:rows], at_last[:rows]
        sums = []
        for t in range(TILES):
            in_y = jnp.where(is_last, up[t + 1], up[t]) + jnp.where(is_first, down[t], down[t + 1])
            in_z = ref[z + 1, t, pl.ds(start, rows), :] + ref[z - 1, t, pl.ds(start, rows), :]
            in_x = ref[z, t, pl.ds(start + 1, rows), :] + ref[z, t, pl.ds(start - 1, rows), :]
            sums.append((in_z + in_x) + in_y)
        return centre, sums

    for kind, field in ((0, ME), (1, MH)):
        arrived(field)

        def roots(z, _, kind=kind, field=field):
            in_z = layer_in(z, SWEEP_HALO)
            halo_mask = halo_inside * in_z
            for t in range(TILES):
                m = land[field][z, pl.ds(0, OWN), pl.ds(128 * t, 128)]
                rs = lax.rsqrt(m)
                rs_buf[kind, z, t] = rs
                s_buf[kind, z, t, pl.ds(FIRST, OWN), :] = (m * rs) * in_z
                m = land[field][z, pl.ds(OWN, 8), pl.ds(128 * t, 128)]
                s = (m * lax.rsqrt(m)) * halo_mask
                s_buf[kind, z, t, pl.ds(0, 8), :] = s
                s_buf[kind, z, t, pl.ds(FIRST + OWN, 8), :] = s
            return 0

        lax.fori_loop(0, NZ + 2 * SWEEP_HALO, roots, 0, unroll=2)

    for kind in (0, 1):

        def stays(z, _, kind=kind):
            centre, sums = around(s_buf.at[kind], z, TOP, NR)
            for t in range(TILES):
                a_buf[kind, z, t, pl.ds(TOP, NR), :] = 1.0 - centre[t] * sums[t]
            return 0

        lax.fori_loop(1, NZ + 2 * SWEEP_HALO - 1, stays, 0, unroll=3)

    arrived(CFL)
    arrived(FRAC)
    arrived(E)
    arrived(H)

    @pl.when(lo_end)
    def _():
        for z in range(UP):
            land[E][z] = jnp.zeros((NR, 2 * NL), jnp.float32)

    @pl.when(hi_end)
    def _():
        for z in range(SWEEP_HALO + NZ, SWEEP_HALO + NZ + UP):
            land[H][z] = jnp.zeros((NR, 2 * NL), jnp.float32)

    layers = NZ + 2 * SWEEP_HALO
    for half in range(2):
        rows = pl.ds(8 * half, 8)
        target_rows = pl.ds(FIRST + 8 * half, 8)

        def drift(t, _, half=half, rows=rows, target_rows=target_rows):
            tile = pl.ds(pl.multiple_of(t * 128, 128), 128)
            d = land[CFL][rows, tile]
            f = land[FRAC][rows, tile]
            rest = 1.0 - f
            bits = [(k, jnp.bitwise_and(d, k) != 0) for k in (8, 4, 2, 1)]
            for kind, field in ((0, E), (1, H)):
                length = layers + UP - 2
                if kind == 0:
                    v = [land[field][length - 1 - i, rows, tile] for i in range(length)]
                else:
                    v = [land[field][i, rows, tile] for i in range(length)]
                for k, bit in bits:
                    if k == 8:
                        v = [jnp.where(bit, v[i + 8], v[i]) if i <= layers else v[i] for i in range(length - 1)]
                    else:
                        v = [jnp.where(bit, v[i + k], v[i]) for i in range(len(v) - k)]
                for i in range(layers):
                    z = layers - 1 - i if kind == 0 else i
                    n = rest * v[i] + f * v[i + 1]
                    q = n * s_buf[kind, z, t, target_rows, :]
                    q0[kind, z, t, target_rows, :] = q
                    if half == 1:
                        q0[kind, z, t, pl.ds(0, 8), :] = q
            return 0

        lax.fori_loop(0, TILES, drift, 0)

    def sweep_one(z, _):
        for kind in (0, 1):
            centre, sums = around(q0.at[kind], z, TOP, NR)
            for t in range(TILES):
                s = s_buf[kind, z, t, pl.ds(TOP, NR), :]
                q1[kind, z, t, pl.ds(TOP, NR), :] = centre[t] * a_buf[kind, z, t, pl.ds(TOP, NR), :] + (s * s) * sums[t]
        return 0

    lax.fori_loop(1, layers - 1, sweep_one, 0, unroll=2)

    arrived(DOP)
    own = pl.ds(FIRST, OWN)

    def sweep_two(z, _):
        found = []
        for kind in (0, 1):
            centre, sums = around(q1.at[kind], z + SWEEP_HALO, FIRST, OWN)
            n = []
            for t in range(TILES):
                s = s_buf[kind, z + SWEEP_HALO, t, own, :]
                q = centre[t] * a_buf[kind, z + SWEEP_HALO, t, own, :] + (s * s) * sums[t]
                n.append(q * rs_buf[kind, z + SWEEP_HALO, t])
                stage[kind, z, :, pl.ds(128 * t, 128)] = n[t]
            found.append(n)
        for t in range(TILES):
            doping = land[DOP][z, :, pl.ds(128 * t, 128)]
            c_buf[z + 3, t, own, :] = (found[1][t] - found[0][t] + doping) * (0.5 / 6.0)
        return 0

    lax.fori_loop(0, NZ, sweep_two, 0, unroll=2)

    copies = []

    def share(src, dst, target):
        k = len(copies)
        copy = pltpu.make_async_remote_copy(
            src_ref=src,
            dst_ref=dst,
            send_sem=c_send.at[k],
            recv_sem=c_recv.at[k],
            device_id=target,
            device_id_type=MESH,
        )
        copy.start()
        copies.append(copy)

    right_dx, left_dx = c, c - 1
    for src_z, dst_z, size, dz in ((3 + NZ - 2, 1, 2, 1), (3, 3 + NZ, 2, -1)):
        for dx, src_x, dst_x in ((right_dx, FIRST + OWN - 2, FIRST - 2), (left_dx, FIRST, FIRST + OWN)):
            share(
                c_buf.at[pl.ds(src_z, size), :, pl.ds(src_x, 2), :],
                c_buf.at[pl.ds(dst_z, size), :, pl.ds(dst_x, 2), :],
                at(dz, dx, 1 - c),
            )
    for dx, src_x, dst_x in ((right_dx, FIRST + OWN - 3, FIRST - 3), (left_dx, FIRST, FIRST + OWN)):
        share(
            c_buf.at[pl.ds(3, NZ), :, pl.ds(src_x, 3), :],
            c_buf.at[pl.ds(3, NZ), :, pl.ds(dst_x, 3), :],
            at(0, dx, 1 - c),
        )
    for src_z, dst_z, dz in ((NZ, 0, 1), (3, 3 + NZ, -1)):
        share(
            c_buf.at[pl.ds(src_z, 3), :, pl.ds(FIRST, OWN), :],
            c_buf.at[pl.ds(dst_z, 3), :, pl.ds(FIRST, OWN), :],
            at(dz, 0, c),
        )

    def give(index):
        mine = pl.ds(pl.multiple_of(c * OWN, OWN), OWN)
        others = pl.ds(pl.multiple_of((1 - c) * NL, NL), NL)
        pltpu.make_async_remote_copy(
            src_ref=stage.at[index, :, :, others],
            dst_ref=outs[index].at[:, mine, :],
            send_sem=o_send.at[index, 0],
            recv_sem=o_recv.at[index],
            device_id=at(0, 0, 1 - c),
            device_id_type=MESH,
        ).start()
        pltpu.make_async_copy(stage.at[index, :, :, lanes], outs[index].at[:, mine, :], o_send.at[index, 1]).start()

    give(0)
    give(1)

    arrived(PHI)

    def spread(z, _):
        in_z = layer_in(z, 4)
        halo_mask = halo_inside * in_z
        for t in range(TILES):
            u_a[z, t, own, :] = land[PHI][z, pl.ds(0, OWN), pl.ds(128 * t, 128)] * in_z
            halo = land[PHI][z, pl.ds(OWN, 8), pl.ds(128 * t, 128)] * halo_mask
            u_a[z, t, pl.ds(0, 8), :] = halo
            u_a[z, t, pl.ds(FIRST + OWN, 8), :] = halo
        return 0

    lax.fori_loop(0, NZ + 8, spread, 0, unroll=2)

    def sweep(src, dst, below, start, stop, charge=None):
        def body(z, _):
            _, sums = around(src, z, TOP, NR)
            weight = inside * (layer_in(z, below) * (1.0 / 6.0))
            for t in range(TILES):
                value = sums[t] * weight
                if charge is not None:
                    value = value + charge[z, t, pl.ds(TOP, NR), :]
                dst[z, t, pl.ds(TOP, NR), :] = value
            return 0

        lax.fori_loop(start, stop, body, 0, unroll=2)

    sweep(u_a, u_b, 4, 1, NZ + 7)
    sweep(u_b, u_a, 4, 2, NZ + 6)
    sweep(u_a, u_b, 4, 3, NZ + 5)

    def sweep_four(z, _):
        _, sums = around(u_b, z + 4, FIRST, OWN)
        for t in range(TILES):
            u_a[z, t, own, :] = sums[t] * (1.0 / 6.0)
        return 0

    lax.fori_loop(0, NZ, sweep_four, 0, unroll=2)

    for copy in copies:
        copy.wait_recv()

    @pl.when(lo_end)
    def _():
        for z in range(3):
            c_buf[z] = jnp.zeros((TILES, ROWS, 128), jnp.float32)

    @pl.when(hi_end)
    def _():
        for z in range(3 + NZ, 6 + NZ):
            c_buf[z] = jnp.zeros((TILES, ROWS, 128), jnp.float32)

    @pl.when(out_left)
    def _():
        for z in range(NZ + 6):
            c_buf[z, :, pl.ds(TOP, OFF), :] = jnp.zeros((TILES, OFF, 128), jnp.float32)

    @pl.when(out_right)
    def _():
        for z in range(NZ + 6):
            c_buf[z, :, pl.ds(FIRST + OWN, OFF), :] = jnp.zeros((TILES, OFF, 128), jnp.float32)

    sweep(c_buf, v_a, 3, 1, NZ + 5, c_buf)
    sweep(v_a, v_b, 3, 2, NZ + 4, c_buf)

    def last_sweep(z, _):
        _, sums = around(v_b, z + 3, FIRST, OWN)
        for t in range(TILES):
            stage[2, z, :, pl.ds(128 * t, 128)] = (sums[t] * (1.0 / 6.0) + c_buf[z + 3, t, own, :]) + u_a[z, t, own, :]
        return 0

    lax.fori_loop(0, NZ, last_sweep, 0, unroll=2)
    give(2)

    for copy in copies:
        copy.wait_send()
    for field in REACH:
        for dz in (-1, 0, 1):
            rows = sent_rows(field, dz)
            if rows:
                view = count.at[pl.ds(0, TILES // 2 * rows), :]
                pltpu.make_async_copy(view, view, in_send.at[field, dz + 1]).wait()
    for index in range(3):
        view = stage.at[index, :, :, pl.ds(0, NL)]
        for sem in (o_send.at[index, 0], o_send.at[index, 1], o_recv.at[index]):
            pltpu.make_async_copy(view, view, sem).wait()


def on_device(sizes, *fields):
    most = max(2 * max(received_rows(field), sent_rows(field, -1), sent_rows(field, 1)) for field in REACH)
    most = 2 * max(most, max(sent_rows(field, 0) for field in REACH))
    landing = [
        pltpu.VMEM(
            (NR, 2 * NL) if field in FLAT else (NZ + below + above, NR if rows else OWN, 2 * NL), fields[field].dtype
        )
        for field, (rows, below, above) in REACH.items()
    ]

    def work(*shape):
        return pltpu.VMEM(shape + (TILES, ROWS, 128), jnp.float32)

    dma = pltpu.SemaphoreType.DMA
    return pl.pallas_call(
        lambda *refs: kernel(sizes, *refs),
        out_shape=[jax.ShapeDtypeStruct((NZ, NR, NL), jnp.float32)] * 3,
        in_specs=[pl.BlockSpec(memory_space=pl.ANY)] * 8,
        out_specs=[pl.BlockSpec(memory_space=pl.ANY)] * 3,
        scratch_shapes=landing
        + [
            work(2, NZ + 4),
            pltpu.VMEM((2, NZ + 4, TILES, OWN, 128), jnp.float32),
            work(2, NZ + 4),
            work(2, NZ + 4),
            work(2, NZ + 4),
            work(NZ + 6),
            work(NZ + 6),
            work(NZ + 6),
            work(NZ + 8),
            work(NZ + 8),
            pltpu.VMEM((3, NZ, OWN, 2 * NL), jnp.float32),
            pltpu.VMEM((most, 128), jnp.float32),
            dma((8, 3)),
            dma((8,)),
            dma((8,)),
            dma((8,)),
            dma((3, 2)),
            dma((3,)),
        ],
        compiler_params=pltpu.CompilerParams(collective_id=0, has_side_effects=True, vmem_limit_bytes=48 << 20),
    )(*fields)


def solution(mesh):
    sizes = (mesh.shape["gz"], mesh.shape["gx"])
    in_specs = (P("gz", "gx", "gy"),) * 6 + (P("gx", "gy"),) * 2
    out_specs = (P("gz", "gx", "gy"),) * 3

    def step(
        electron_density, hole_density, potential, doping, electron_mobility, hole_mobility, cfl_map, fraction
    ):
        return tuple(
            on_device(
                sizes, electron_density, hole_density, electron_mobility, hole_mobility, potential, doping, cfl_map,
                fraction,
            )
        )

    return jax.shard_map(step, mesh=mesh, in_specs=in_specs, out_specs=out_specs, check_vma=False)
```

time: 189 us -> 50.3 us (0.27)
  the two profiles are of different devices: /device:TPU:51 before, /device:TPU:1 now
where the time goes in v1:
time: 50.3 us; the launch traced here: 49.9 us
  Pallas kernels  40 us (80%)
  local copies, waits for them, and re-layouts  9.23 us (18%)
  between operations  0.66 us (1%)
    pallas_call x1, Pallas kernels, on_device(): pl.pallas_call(lambda *refs: kernel(sizes, *refs), out_shape=[jax.ShapeDt...  40 us
    unnamed x19, local copies, waits for them, and re-layouts  9.23 us

profile of v1, /device:TPU:1, one launch (start us, length us, event | category | flops | bytes accessed | tf_op | source)
XLA Modules:
  0.0 49.9 jit_solution(5831632118954134820)
XLA Ops:
  0.6 0.0 copy-start
  0.6 0.9 %copy-done = f32[16,16,256]{2,1,0:T(8,128)S(1)} copy-done((f32[16,16,256]{2,1,0:T(8,128)S(1)}, f32[16,16,256]{2,1,0:T(8,128)}, u32[]{:S(2)}) %copy-start) | copy-done | bytes 262168
  1.6 0.0 copy-start.1
  1.6 0.9 %copy-done.1 = f32[16,16,256]{2,1,0:T(8,128)S(1)} copy-done((f32[16,16,256]{2,1,0:T(8,128)S(1)}, f32[16,16,256]{2,1,0:T(8,128)}, u32[]{:S(2)}) %copy-start.1) | copy-done | bytes 262168
  2.5 0.0 copy-start.2
  2.5 0.9 %copy-done.2 = f32[16,16,256]{2,1,0:T(8,128)S(1)} copy-done((f32[16,16,256]{2,1,0:T(8,128)S(1)}, f32[16,16,256]{2,1,0:T(8,128)}, u32[]{:S(2)}) %copy-start.2) | copy-done | bytes 262168
  3.5 0.0 copy-start.3
  3.5 0.9 %copy-done.3 = f32[16,16,256]{2,1,0:T(8,128)S(1)} copy-done((f32[16,16,256]{2,1,0:T(8,128)S(1)}, f32[16,16,256]{2,1,0:T(8,128)}, u32[]{:S(2)}) %copy-start.3) | copy-done | bytes 262168
  4.4 0.0 copy-start.4
  4.4 0.9 %copy-done.4 = f32[16,16,256]{2,1,0:T(8,128)S(1)} copy-done((f32[16,16,256]{2,1,0:T(8,128)S(1)}, f32[16,16,256]{2,1,0:T(8,128)}, u32[]{:S(2)}) %copy-start.4) | copy-done | bytes 262168
  5.4 0.0 copy-start.5
  5.4 0.9 %copy-done.5 = f32[16,16,256]{2,1,0:T(8,128)S(1)} copy-done((f32[16,16,256]{2,1,0:T(8,128)S(1)}, f32[16,16,256]{2,1,0:T(8,128)}, u32[]{:S(2)}) %copy-start.5) | copy-done | bytes 262168
  6.3 0.0 copy-start.6
  6.3 0.7 %copy-done.6 = s32[16,256]{1,0:T(8,128)S(1)} copy-done((s32[16,256]{1,0:T(8,128)S(1)}, s32[16,256]{1,0:T(8,128)}, u32[]{:S(2)}) %copy-start.6) | copy-done | bytes 16408
  7.1 0.0 copy-start.7
  7.1 0.7 %copy-done.7 = f32[16,256]{1,0:T(8,128)S(1)} copy-done((f32[16,256]{1,0:T(8,128)S(1)}, f32[16,256]{1,0:T(8,128)}, u32[]{:S(2)}) %copy-start.7) | copy-done | bytes 16408
  7.8 40.0 %shard_map.103 = (f32[16,16,256]{2,1,0:T(8,128)S(1)}, f32[16,16,256]{2,1,0:T(8,128)S(1)}, f32[16,16,256]{2,1,0:T(8,128)S(1)}) custom-call(f32[16,16,256]{2,1,0:T(8,128)S(1)} %copy-done, f32[16,16,256]{2,1,0:T(8,128)S(1)} %copy-done.1, f32[16,16,256]{2,1,0:T(8,128)S(1)} %copy-done.2, f32[16,16,256]{2,1,0:T(8,128)S(1)} %copy-done.3, ...), custom_call_target="tpu_custom_call" | custom-call | tf_op jit(solution)/shard_map/pallas_call | solution.py:460
  47.8 0.7 %copy.14 = f32[16,16,256]{2,1,0:T(8,128)} copy(f32[16,16,256]{2,1,0:T(8,128)S(1)} %get-tuple-element.6) | data formatting | bytes 524288
  48.5 0.7 %copy.15 = f32[16,16,256]{2,1,0:T(8,128)} copy(f32[16,16,256]{2,1,0:T(8,128)S(1)} %get-tuple-element.7) | data formatting | bytes 524288
  49.2 0.7 %copy.16 = f32[16,16,256]{2,1,0:T(8,128)} copy(f32[16,16,256]{2,1,0:T(8,128)S(1)} %get-tuple-element.8) | data formatting | bytes 524288
Async XLA Ops:
  0.6 1.0 %copy-start = (f32[16,16,256]{2,1,0:T(8,128)S(1)}, f32[16,16,256]{2,1,0:T(8,128)}, u32[]{:S(2)}) copy-start(f32[16,16,256]{2,1,0:T(8,128)} %refs_0_.1) | copy-start | bytes 786436
  1.6 0.9 %copy-start.1 = (f32[16,16,256]{2,1,0:T(8,128)S(1)}, f32[16,16,256]{2,1,0:T(8,128)}, u32[]{:S(2)}) copy-start(f32[16,16,256]{2,1,0:T(8,128)} %refs_1_.1) | copy-start | bytes 786436
  2.5 0.9 %copy-start.2 = (f32[16,16,256]{2,1,0:T(8,128)S(1)}, f32[16,16,256]{2,1,0:T(8,128)}, u32[]{:S(2)}) copy-start(f32[16,16,256]{2,1,0:T(8,128)} %refs_2_.1) | copy-start | bytes 786436
  3.5 0.9 %copy-start.3 = (f32[16,16,256]{2,1,0:T(8,128)S(1)}, f32[16,16,256]{2,1,0:T(8,128)}, u32[]{:S(2)}) copy-start(f32[16,16,256]{2,1,0:T(8,128)} %refs_3_.1) | copy-start | bytes 786436
  4.4 0.9 %copy-start.4 = (f32[16,16,256]{2,1,0:T(8,128)S(1)}, f32[16,16,256]{2,1,0:T(8,128)}, u32[]{:S(2)}) copy-start(f32[16,16,256]{2,1,0:T(8,128)} %refs_4_.1) | copy-start | bytes 786436
  5.4 0.9 %copy-start.5 = (f32[16,16,256]{2,1,0:T(8,128)S(1)}, f32[16,16,256]{2,1,0:T(8,128)}, u32[]{:S(2)}) copy-start(f32[16,16,256]{2,1,0:T(8,128)} %refs_5_.1) | copy-start | bytes 786436
  6.3 0.7 %copy-start.6 = (s32[16,256]{1,0:T(8,128)S(1)}, s32[16,256]{1,0:T(8,128)}, u32[]{:S(2)}) copy-start(s32[16,256]{1,0:T(8,128)} %refs_6_.1) | copy-start | bytes 49156
  7.1 0.7 %copy-start.7 = (f32[16,256]{1,0:T(8,128)S(1)}, f32[16,256]{1,0:T(8,128)}, u32[]{:S(2)}) copy-start(f32[16,256]{1,0:T(8,128)} %refs_7_.1) | copy-start | bytes 49156

commit v2 on v0

v2 whole, which is shorter than its diff:
```python
import jax
import jax.numpy as jnp
from jax import lax
from jax.experimental import pallas as pl
from jax.experimental.pallas import tpu as pltpu
from jax.sharding import PartitionSpec as P

MESH = pl.DeviceIdType.MESH

CFL_MAX = 8
NZ = 16
NX = 16
NL = 256
OWN = 8
TILES = 4
ROWS = 32
FIRST = 8
LANDING = 24
TOP, SPAN = 4, 24
CHARGE = 3
SWEEPS = 4
DIFFUSION = 2
UP = CFL_MAX + 1 + DIFFUSION
LAYERS = OWN + 2 * DIFFUSION
SEAM = 8

E, H, ME, MH, PHI, DOP, CFL, FRAC = range(8)
REACH = {
    E: (DIFFUSION, UP, DIFFUSION),
    H: (DIFFUSION, DIFFUSION, UP),
    ME: (DIFFUSION, DIFFUSION, DIFFUSION),
    MH: (DIFFUSION, DIFFUSION, DIFFUSION),
    PHI: (SWEEPS, SWEEPS, SWEEPS),
    DOP: (0, 0, 0),
    CFL: (DIFFUSION, 0, 0),
    FRAC: (DIFFUSION, 0, 0),
}
FLAT = (CFL, FRAC)
GROUPS = ((ME, MH), (E, H, CFL, FRAC), (DOP,), (PHI,))
MOBILITIES, DENSITIES, DOPING, POTENTIAL = range(4)
SIDES = [(dz, dx) for dz in (1, -1, 0) for dx in (1, -1, 0)]


def piece(field, core, dz, dx):
    rows, below, above = REACH[field]
    if field in FLAT:
        along_z = (0, 0, 1 if dz == 0 else 0)
    else:
        start, stop = OWN * core - below, OWN * core + OWN + above
        if dz == 0:
            along_z = (max(start, 0), max(-start, 0), min(stop, NZ) - max(start, 0))
        elif dz == 1:
            along_z = (NZ + start, 0, -start)
        else:
            along_z = (0, NZ - start, stop - NZ)
    along_x = {0: (0, 0, NX), 1: (NX - rows, LANDING - rows, rows), -1: (0, NX, rows)}[dx]
    return (along_z, along_x) if along_z[2] > 0 and along_x[2] > 0 else None


def received(group, core, side):
    pieces = [piece(field, core, *side) for field in GROUPS[group]]
    return sum(TILES * p[0][2] * p[1][2] for p in pieces if p is not None)


def sent(side):
    total = 0
    for field in REACH:
        for core in (0, 1):
            p = piece(field, core, *side)
            if p is not None:
                total += TILES // 2 * p[0][2] * p[1][2]
    return total // 2 if side == (0, 0) else total


def kernel(sizes, *refs):
    n_gz, n_gx = sizes
    ins, outs, land = refs[:8], refs[8:11], refs[11:19]
    (s_buf, rs_buf, a_buf, q0, q1, result, c_buf, v_a, v_b, u_a, u_b, count, late, in_send, in_recv, c_send, c_recv, o_send,
     o_recv) = refs[19:]
    g, w, c = lax.axis_index("gz"), lax.axis_index("gx"), lax.axis_index("gy")
    lowest, highest, leftmost, rightmost = g == 0, g == n_gz - 1, w == 0, w == n_gx - 1

    def at(dz, dx, core):
        return (g + dz, w + dx, core)

    def both(*conditions):
        result = None
        for condition in conditions:
            if condition is not None:
                result = condition if result is None else jnp.logical_and(result, condition)
        return result

    def exists(dz, dx):
        return both(
            {1: jnp.logical_not(highest), -1: jnp.logical_not(lowest), 0: None}[dz],
            {1: jnp.logical_not(rightmost), -1: jnp.logical_not(leftmost), 0: None}[dx],
        )

    def when(condition, body):
        if condition is None:
            body()
        else:
            pl.when(condition)(body)

    seam_left = jnp.logical_and(lax.rem(w, SEAM) == 0, jnp.logical_not(leftmost))
    seam_right = jnp.logical_and(lax.rem(w, SEAM) == SEAM - 1, jnp.logical_not(rightmost))
    barrier = pltpu.get_barrier_semaphore()

    def greet(semaphore, dz, dx):
        if (dz, dx) == (0, 0):
            pl.semaphore_signal(semaphore, inc=1, device_id=at(0, 0, 1 - c), device_id_type=MESH)
        else:
            for core in (0, 1):
                pl.semaphore_signal(semaphore, inc=1, device_id=at(dz, dx, core), device_id_type=MESH)

    for dz, dx in SIDES:
        open_side = jnp.logical_not(seam_right) if dx == 1 else None
        when(both(exists(dz, dx), open_side), lambda dz=dz, dx=dx: greet(barrier, dz, dx))
    deep = 3 - lowest.astype(jnp.int32) - highest.astype(jnp.int32)
    wide = 3 - jnp.logical_or(leftmost, seam_left).astype(jnp.int32) - rightmost.astype(jnp.int32)
    pl.semaphore_wait(barrier, 2 * deep * wide - 1)
    for dz in (1, -1, 0):
        when(both(exists(dz, 1), seam_right), lambda dz=dz: greet(late, dz, 1))

    lanes = pl.ds(pl.multiple_of(c * NL, NL), NL)

    def push(group, side):
        dz, dx = side
        for field in GROUPS[group]:
            for core in (0, 1):
                p = piece(field, core, dz, dx)
                if p is None:
                    continue
                (src_z, dst_z, depth), (src_x, dst_x, rows) = p
                if field in FLAT:
                    src = ins[field].at[pl.ds(src_x, rows), :]
                    dst = land[field].at[pl.ds(dst_x, rows), lanes]
                else:
                    src = ins[field].at[pl.ds(src_z, depth), pl.ds(src_x, rows), :]
                    dst = land[field].at[pl.ds(dst_z, depth), pl.ds(dst_x, rows), lanes]
                sem = in_recv.at[group, 3 * dz + dx + 4]

                def remote(src=src, dst=dst, sem=sem, core=core):
                    pltpu.make_async_remote_copy(
                        src_ref=src,
                        dst_ref=dst,
                        send_sem=in_send.at[3 * dz + dx + 4],
                        recv_sem=sem,
                        device_id=at(dz, dx, core),
                        device_id_type=MESH,
                    ).start()

                def local(src=src, dst=dst, sem=sem):
                    pltpu.make_async_copy(src, dst, sem).start()

                if side == (0, 0):
                    pl.when(c == core)(local)
                    pl.when(c != core)(remote)
                else:
                    remote()

    def push_all(group, sides, condition=None):
        for side in sides:
            when(both(exists(*side), condition), lambda side=side: push(group, side))

    def wait_rows(rows, sem):
        view = count.at[pl.ds(0, rows), :]
        pltpu.make_async_copy(view, view, sem).wait()

    def arrived(group):
        for dz, dx in SIDES:
            for core in (0, 1):
                rows = received(group, core, (dz, dx))
                if rows == 0:
                    continue
                even = core == 1 or received(group, 1, (dz, dx)) != rows
                if core == 1 and received(group, 0, (dz, dx)) == rows:
                    continue
                mine = c == core if even else None
                sem = in_recv.at[group, 3 * dz + dx + 4]
                when(both(exists(-dz, -dx), mine), lambda rows=rows, sem=sem: wait_rows(rows, sem))

    right = [(dz, 1) for dz in (1, -1, 0)]
    left = [(dz, -1) for dz in (1, -1, 0)]
    near = [(1, 0), (-1, 0), (0, 0)]
    for group in range(4):
        push_all(group, right)
        push_all(group, left, jnp.logical_not(seam_left))
        push_all(group, near)

    @pl.when(seam_left)
    def _():
        pl.semaphore_wait(late, 2 * deep)
        for group in range(4):
            push_all(group, left)

    def splat(flag, rows):
        return jnp.broadcast_to(flag.astype(jnp.int32), (rows, 128)) > 0

    has_left, has_right = jnp.logical_not(leftmost), jnp.logical_not(rightmost)
    row = lax.broadcasted_iota(jnp.int32, (SPAN, 128), 0) + (TOP - FIRST)
    first_row = jnp.where(leftmost, 0, -FIRST)
    last_row = jnp.where(rightmost, NX, NX + FIRST)
    inside = jnp.logical_and(row >= first_row, row < last_row)
    sixth = jnp.where(inside, 1.0 / 6.0, 0.0)
    halo_row = lax.broadcasted_iota(jnp.int32, (8, 128), 0)
    halo_inside = jnp.where(halo_row < 4, has_right.astype(jnp.int32), has_left.astype(jnp.int32))
    lane = lax.broadcasted_iota(jnp.int32, (SPAN, 128), 1)
    at_first, at_last = lane == 0, lane == 127

    def layer_in(z, below):
        z = z - below + OWN * c
        return jnp.logical_and(jnp.logical_or(z >= 0, jnp.logical_not(lowest)), jnp.logical_or(z < NZ, jnp.logical_not(highest)))

    def around(ref, z, start, rows):
        centre = [ref[z, t, pl.ds(start, rows), :] for t in range(TILES)]
        up = [pltpu.roll(v, 127, 1) for v in centre] + [jnp.zeros((rows, 128), jnp.float32)]
        down = [jnp.zeros((rows, 128), jnp.float32)] + [pltpu.roll(v, 1, 1) for v in centre]
        is_first, is_last = at_first[:rows], at_last[:rows]
        sums = []
        for t in range(TILES):
            in_y = jnp.where(is_last, up[t + 1], up[t]) + jnp.where(is_first, down[t], down[t + 1])
            in_z = ref[z + 1, t, pl.ds(start, rows), :] + ref[z - 1, t, pl.ds(start, rows), :]
            in_x = ref[z, t, pl.ds(start + 1, rows), :] + ref[z, t, pl.ds(start - 1, rows), :]
            sums.append((in_z + in_x) + in_y)
        return centre, sums

    def empty(field, start, layers):
        for z in range(start, start + layers):
            land[field][z] = jnp.zeros((LANDING, 2 * NL), jnp.float32)

    for core in (0, 1):

        @pl.when(jnp.logical_and(lowest, c == core))
        def _(core=core):
            empty(E, 0, UP - OWN * core)
            if core == 0:
                empty(H, 0, DIFFUSION)

        @pl.when(jnp.logical_and(highest, c == core))
        def _(core=core):
            empty(H, DIFFUSION + NZ - OWN * core, UP - OWN * (1 - core))
            if core == 1:
                empty(E, UP + OWN, DIFFUSION)

    arrived(MOBILITIES)
    own, halo = pl.ds(FIRST, NX), pl.ds(NX, 8)
    after, before = pl.ds(FIRST + NX, 8), pl.ds(0, 8)

    def roots(z, _):
        in_z = layer_in(z, DIFFUSION).astype(jnp.int32)
        own_mask, halo_mask = jnp.broadcast_to(in_z, (NX, 128)) > 0, halo_inside * in_z > 0
        for kind, field in ((0, ME), (1, MH)):
            for t in range(TILES):
                m = land[field][z, pl.ds(0, NX), pl.ds(128 * t, 128)]
                rs = lax.rsqrt(m)
                rs_buf[kind, z, t] = rs
                s_buf[kind, z, t, own, :] = jnp.where(own_mask, m * rs, 0.0)
                m = land[field][z, halo, pl.ds(128 * t, 128)]
                s = jnp.where(halo_mask, m * lax.rsqrt(m), 0.0)
                s_buf[kind, z, t, before, :] = s
                s_buf[kind, z, t, after, :] = s
        return 0

    lax.fori_loop(0, LAYERS, roots, 0)

    def stays(z, _):
        for kind in (0, 1):
            centre, sums = around(s_buf.at[kind], z, TOP, SPAN)
            for t in range(TILES):
                a_buf[kind, z, t, pl.ds(TOP, SPAN), :] = 1.0 - centre[t] * sums[t]
        return 0

    lax.fori_loop(1, LAYERS - 1, stays, 0)

    arrived(DENSITIES)
    for from_row, to_row in ((0, 8), (8, 16), (16, 24)):
        rows, target = pl.ds(from_row, 8), pl.ds(to_row, 8)

        def drift(t, _, rows=rows, target=target, at_halo=from_row == NX):
            tile = pl.ds(pl.multiple_of(t * 128, 128), 128)
            d = land[CFL][rows, tile]
            f = land[FRAC][rows, tile]
            rest = 1.0 - f
            bits = [(k, jnp.bitwise_and(d, k) != 0) for k in (8, 4, 2, 1)]
            mask = halo_inside > 0
            for kind, field in ((0, E), (1, H)):
                length = LAYERS + CFL_MAX + 1
                if kind == 0:
                    v = [land[field][length - 1 - i, rows, tile] for i in range(length)]
                else:
                    v = [land[field][i, rows, tile] for i in range(length)]
                for k, bit in bits:
                    if k == 8:
                        v = [jnp.where(bit, v[i + 8], v[i]) if i <= LAYERS else v[i] for i in range(length - 1)]
                    else:
                        v = [jnp.where(bit, v[i + k], v[i]) for i in range(len(v) - k)]
                for i in range(LAYERS):
                    z = LAYERS - 1 - i if kind == 0 else i
                    q = (rest * v[i] + f * v[i + 1]) * s_buf[kind, z, t, target, :]
                    if at_halo:
                        q = jnp.where(mask, q, 0.0)
                        q0[kind, z, t, before, :] = q
                    q0[kind, z, t, target, :] = q
            return 0

        lax.fori_loop(0, TILES, drift, 0)

    span = pl.ds(TOP, SPAN)

    def sweep_one(z, _):
        for kind in (0, 1):
            centre, sums = around(q0.at[kind], z, TOP, SPAN)
            for t in range(TILES):
                s = s_buf[kind, z, t, span, :]
                q1[kind, z, t, span, :] = centre[t] * a_buf[kind, z, t, span, :] + (s * s) * sums[t]
        return 0

    lax.fori_loop(1, LAYERS - 1, sweep_one, 0)

    arrived(DOPING)

    def sweep_two(z, _):
        found = []
        for kind in (0, 1):
            centre, sums = around(q1.at[kind], z + DIFFUSION, FIRST, NX)
            n = []
            for t in range(TILES):
                s = s_buf[kind, z + DIFFUSION, t, own, :]
                q = centre[t] * a_buf[kind, z + DIFFUSION, t, own, :] + (s * s) * sums[t]
                n.append(q * rs_buf[kind, z + DIFFUSION, t])
                result[kind, z, t, own, :] = n[t]
            found.append(n)
        for t in range(TILES):
            doping = land[DOP][z, pl.ds(0, NX), pl.ds(128 * t, 128)]
            c_buf[z + CHARGE, t, own, :] = (found[1][t] - found[0][t] + doping) * (0.5 / 6.0)
        return 0

    lax.fori_loop(0, OWN, sweep_two, 0)

    above_there, below_there = jnp.logical_or(c == 0, jnp.logical_not(highest)), jnp.logical_or(c == 1, jnp.logical_not(lowest))
    upward, downward = c, c - 1

    def exchange(ways, start):
        for dz, dx in ways:
            depth, rows = (CHARGE, NX) if dx == 0 else (CHARGE - 1, CHARGE - 1) if dz != 0 else (OWN, CHARGE)
            src_z, dst_z = {1: (CHARGE + OWN - depth, CHARGE - depth), -1: (CHARGE, CHARGE + OWN), 0: (CHARGE, CHARGE)}[dz]
            src_x, dst_x = {1: (FIRST + NX - rows, FIRST - rows), -1: (FIRST, FIRST + NX), 0: (FIRST, FIRST)}[dx]
            way = 3 * dz + dx + 4
            chip = {1: upward, -1: downward, 0: 0}[dz]
            core = c if dz == 0 else 1 - c

            def one(src_z=src_z, dst_z=dst_z, src_x=src_x, dst_x=dst_x, depth=depth, rows=rows, way=way, chip=chip, core=core, dx=dx):
                copy = pltpu.make_async_remote_copy(
                    src_ref=c_buf.at[pl.ds(src_z, depth), :, pl.ds(src_x, rows), :],
                    dst_ref=c_buf.at[pl.ds(dst_z, depth), :, pl.ds(dst_x, rows), :],
                    send_sem=c_send.at[way],
                    recv_sem=c_recv.at[way],
                    device_id=at(chip, dx, core),
                    device_id_type=MESH,
                )
                if start:
                    copy.start()
                else:
                    copy.wait_send()

            when(both({1: above_there, -1: below_there, 0: None}[dz], exists(0, dx)), one)

    def charge_arrived(ways):
        for dz, dx in ways:
            depth, rows = (CHARGE, NX) if dx == 0 else (CHARGE - 1, CHARGE - 1) if dz != 0 else (OWN, CHARGE)
            view = c_buf.at[pl.ds(0, depth), :, pl.ds(0, rows), :]
            way = 3 * dz + dx + 4

            def one(view=view, way=way):
                pltpu.make_async_copy(view, view, c_recv.at[way]).wait()

            when(both({1: below_there, -1: above_there, 0: None}[dz], exists(0, -dx)), one)

    ways = [(1, 1), (-1, 1), (1, -1), (-1, -1), (0, 1), (0, -1), (1, 0), (-1, 0)]
    exchange(ways, True)

    mine = pl.ds(pl.multiple_of(c * OWN, OWN), OWN)

    def give(index):
        for k in range(TILES // 2):
            there = outs[index].at[mine, :, pl.ds(128 * k, 128)]
            pltpu.make_async_remote_copy(
                src_ref=result.at[index, :, 2 * (1 - c) + k, pl.ds(FIRST, NX), :],
                dst_ref=there,
                send_sem=o_send.at[index, k],
                recv_sem=o_recv.at[index, k],
                device_id=at(0, 0, 1 - c),
                device_id_type=MESH,
            ).start()
            pltpu.make_async_copy(result.at[index, :, 2 * c + k, pl.ds(FIRST, NX), :], there, o_send.at[index, 2 + k]).start()

    give(0)
    give(1)

    arrived(POTENTIAL)

    def spread(z, _):
        in_z = layer_in(z, SWEEPS).astype(jnp.int32)
        own_mask, halo_mask = jnp.broadcast_to(in_z, (NX, 128)) > 0, halo_inside * in_z > 0
        for t in range(TILES):
            tile = pl.ds(128 * t, 128)
            u_a[z, t, own, :] = jnp.where(own_mask, land[PHI][z, pl.ds(0, NX), tile], 0.0)
            phi = jnp.where(halo_mask, land[PHI][z, halo, tile], 0.0)
            u_a[z, t, before, :] = phi
            u_a[z, t, after, :] = phi
        return 0

    lax.fori_loop(0, OWN + 2 * SWEEPS, spread, 0)

    def sweep(src, dst, below, start, stop, charge=None):
        def body(z, _):
            _, sums = around(src, z, TOP, SPAN)
            weight = jnp.where(splat(layer_in(z, below), SPAN), sixth, 0.0)
            for t in range(TILES):
                value = sums[t] * weight
                if charge is not None:
                    value = value + charge[z, t, span, :]
                dst[z, t, span, :] = value
            return 0

        lax.fori_loop(start, stop, body, 0, unroll=2)

    sweep(u_a, u_b, SWEEPS, 1, OWN + 2 * SWEEPS - 1)
    sweep(u_b, u_a, SWEEPS, 2, OWN + 2 * SWEEPS - 2)
    sweep(u_a, u_b, SWEEPS, 3, OWN + 2 * SWEEPS - 3)

    def sweep_four(z, _):
        _, sums = around(u_b, z + SWEEPS, FIRST, NX)
        for t in range(TILES):
            u_a[z, t, own, :] = sums[t] * (1.0 / 6.0)
        return 0

    lax.fori_loop(0, OWN, sweep_four, 0, unroll=2)

    def clear(condition, start, layers, first, rows):
        @pl.when(condition)
        def _():
            for z in range(start, start + layers):
                c_buf[z, :, pl.ds(first, rows), :] = jnp.zeros((TILES, rows, 128), jnp.float32)

    clear(jnp.logical_not(below_there), 0, CHARGE, 0, ROWS)
    clear(jnp.logical_not(above_there), CHARGE + OWN, CHARGE, 0, ROWS)
    clear(leftmost, 0, OWN + 2 * CHARGE, TOP, FIRST - TOP)
    clear(rightmost, 0, OWN + 2 * CHARGE, FIRST + NX, FIRST - TOP)
    charge_arrived(ways)

    sweep(c_buf, v_a, CHARGE, 1, OWN + 2 * CHARGE - 1, c_buf)
    sweep(v_a, v_b, CHARGE, 2, OWN + 2 * CHARGE - 2, c_buf)

    def last_sweep(z, _):
        _, sums = around(v_b, z + CHARGE, FIRST, NX)
        for t in range(TILES):
            result[2, z, t, own, :] = (sums[t] * (1.0 / 6.0) + c_buf[z + CHARGE, t, own, :]) + u_a[z, t, own, :]
        return 0

    lax.fori_loop(0, OWN, last_sweep, 0, unroll=2)
    give(2)

    exchange(ways, False)
    for dz, dx in SIDES:
        when(exists(dz, dx), lambda dz=dz, dx=dx: wait_rows(sent((dz, dx)), in_send.at[3 * dz + dx + 4]))
    for index in range(3):
        view = result.at[index, :, 0, own, :]
        for k in range(TILES // 2):
            for sem in (o_send.at[index, k], o_send.at[index, 2 + k], o_recv.at[index, k]):
                pltpu.make_async_copy(view, view, sem).wait()


def hand_over(*refs):
    ins, outs, sems = refs[:3], refs[3:6], refs[6]
    copies = [pltpu.make_async_copy(ins[k], outs[k], sems.at[k]) for k in range(3)]
    for copy in copies:
        copy.start()
    for copy in copies:
        copy.wait()


def on_device(sizes, *fields):
    most = max(max(sent(side), received(group, core, side)) for side in SIDES for group in range(4) for core in (0, 1))
    landing = [
        pltpu.VMEM(
            (LANDING, 2 * NL) if field in FLAT else (OWN + below + above, LANDING if rows else NX, 2 * NL), fields[field].dtype
        )
        for field, (rows, below, above) in REACH.items()
    ]

    def work(*shape):
        return pltpu.VMEM(shape + (TILES, ROWS, 128), jnp.float32)

    dma = pltpu.SemaphoreType.DMA
    shapes = [jax.ShapeDtypeStruct((NZ, NX, NL), jnp.float32)] * 3
    found = pl.pallas_call(
        lambda *refs: kernel(sizes, *refs),
        out_shape=[pltpu.VMEM((NZ, NX, NL), jnp.float32)] * 3,
        in_specs=[pl.BlockSpec(memory_space=pl.ANY)] * 8,
        out_specs=[pl.BlockSpec(memory_space=pl.ANY)] * 3,
        scratch_shapes=landing
        + [
            work(2, LAYERS),
            pltpu.VMEM((2, LAYERS, TILES, NX, 128), jnp.float32),
            work(2, LAYERS),
            work(2, LAYERS),
            work(2, LAYERS),
            work(3, OWN),
            work(OWN + 2 * CHARGE),
            work(OWN + 2 * CHARGE),
            work(OWN + 2 * CHARGE),
            work(OWN + 2 * SWEEPS),
            work(OWN + 2 * SWEEPS),
            pltpu.VMEM((most, 128), jnp.float32),
            pltpu.SemaphoreType.REGULAR,
            dma((9,)),
            dma((4, 9)),
            dma((9,)),
            dma((9,)),
            dma((3, 4)),
            dma((3, 2)),
        ],
        compiler_params=pltpu.CompilerParams(collective_id=0, has_side_effects=True, vmem_limit_bytes=60 << 20),
    )(*fields)
    return pl.pallas_call(
        hand_over,
        out_shape=shapes,
        in_specs=[pl.BlockSpec(memory_space=pl.ANY)] * 3,
        out_specs=[pl.BlockSpec(memory_space=pl.ANY)] * 3,
        scratch_shapes=[dma((3,))],
        compiler_params=pltpu.CompilerParams(vmem_limit_bytes=8 << 20),
    )(*found)


def solution(mesh):
    sizes = (mesh.shape["gz"], mesh.shape["gx"])
    in_specs = (P("gz", "gx", "gy"),) * 6 + (P("gx", "gy"),) * 2
    out_specs = (P("gz", "gx", "gy"),) * 3

    def step(
        electron_density, hole_density, potential, doping, electron_mobility, hole_mobility, cfl_map, fraction
    ):
        return tuple(
            on_device(
                sizes, electron_density, hole_density, electron_mobility, hole_mobility, potential, doping, cfl_map,
                fraction,
            )
        )

    return jax.shard_map(step, mesh=mesh, in_specs=in_specs, out_specs=out_specs, check_vma=False)
```

time: 189 us -> 36.9 us (0.20)
  the two profiles are of different devices: /device:TPU:51 before, /device:TPU:31 now
where the time goes in v2:
time: 36.9 us; the launch traced here: 36.7 us
  Pallas kernels  36.1 us (98%)
  between operations  0.64 us (2%)
    pallas_call x1, Pallas kernels, on_device(): pl.pallas_call(lambda *refs: kernel(sizes, *refs), out_shape=[pltpu.VMEM(...  35.2 us
    pallas_call x1, Pallas kernels, on_device(): pl.pallas_call(hand_over, out_shape=shapes, in_specs=[pl.BlockSpec(memory...  0.9 us

profile of v2, /device:TPU:31, one launch (start us, length us, event | category | flops | bytes accessed | tf_op | source)
XLA Modules:
  0.0 36.7 jit_solution(3208552710461274130)
XLA Ops:
  0.6 35.2 %shard_map.103 = (f32[16,16,256]{2,1,0:T(8,128)S(1)}, f32[16,16,256]{2,1,0:T(8,128)S(1)}, f32[16,16,256]{2,1,0:T(8,128)S(1)}) custom-call(f32[16,16,256]{2,1,0:T(8,128)} %refs_0_.1, f32[16,16,256]{2,1,0:T(8,128)} %refs_1_.1, f32[16,16,256]{2,1,0:T(8,128)} %refs_2_.1, f32[16,16,256]{2,1,0:T(8,128)} %refs_3_.1, f32[16,16,256]{2,1,0:T(8,128)} %refs_4_.1, ...), custom_call_target="tpu_custom_call" | custom-call | tf_op jit(solution)/shard_map/pallas_call | solution.py:498
  35.8 0.9 %shard_map.104 = (f32[16,16,256]{2,1,0:T(8,128)}, f32[16,16,256]{2,1,0:T(8,128)}, f32[16,16,256]{2,1,0:T(8,128)}) custom-call(f32[16,16,256]{2,1,0:T(8,128)S(1)} %get-tuple-element.6.refs_0_, f32[16,16,256]{2,1,0:T(8,128)S(1)} %get-tuple-element.7.refs_1_, f32[16,16,256]{2,1,0:T(8,128)S(1)} %get-tuple-element.8.refs_2_), custom_call_target="tpu_custom_call" | custom-call | tf_op jit(solution)/shard_map/pallas_call | solution.py:527

commit v3 on v2

--- a/solution.py
+++ b/solution.py
@@ -18,7 +18,7 @@
 LANDING = 24
 TOP, SPAN = 4, 24
 CHARGE = 3
-SWEEPS = 4
+EARLY = 2
 DIFFUSION = 2
 UP = CFL_MAX + 1 + DIFFUSION
 LAYERS = OWN + 2 * DIFFUSION
@@ -30,14 +30,14 @@
     H: (DIFFUSION, DIFFUSION, UP),
     ME: (DIFFUSION, DIFFUSION, DIFFUSION),
     MH: (DIFFUSION, DIFFUSION, DIFFUSION),
-    PHI: (SWEEPS, SWEEPS, SWEEPS),
+    PHI: (EARLY, EARLY, EARLY),
     DOP: (0, 0, 0),
     CFL: (DIFFUSION, 0, 0),
     FRAC: (DIFFUSION, 0, 0),
 }
 FLAT = (CFL, FRAC)
-GROUPS = ((ME, MH), (E, H, CFL, FRAC), (DOP,), (PHI,))
-MOBILITIES, DENSITIES, DOPING, POTENTIAL = range(4)
+GROUPS = ((ME, MH), (PHI,), (E, H, CFL, FRAC), (DOP,))
+MOBILITIES, POTENTIAL, DENSITIES, DOPING = range(4)
 SIDES = [(dz, dx) for dz in (1, -1, 0) for dx in (1, -1, 0)]
 
 
@@ -46,13 +46,15 @@
     if field in FLAT:
         along_z = (0, 0, 1 if dz == 0 else 0)
     else:
-        start, stop = OWN * core - below, OWN * core + OWN + above
+        base = OWN * core - below
+        start, stop = base + abs(dx), OWN * core + OWN + above - abs(dx)
         if dz == 0:
-            along_z = (max(start, 0), max(-start, 0), min(stop, NZ) - max(start, 0))
+            start, stop = max(start, 0), min(stop, NZ)
+            along_z = (start, start - base, stop - start)
         elif dz == 1:
-            along_z = (NZ + start, 0, -start)
+            along_z = (NZ + start, start - base, -start)
         else:
-            along_z = (0, NZ - start, stop - NZ)
+            along_z = (0, NZ - base, stop - NZ)
     along_x = {0: (0, 0, NX), 1: (NX - rows, LANDING - rows, rows), -1: (0, NX, rows)}[dx]
     return (along_z, along_x) if along_z[2] > 0 and along_x[2] > 0 else None
 
@@ -75,8 +77,8 @@
 def kernel(sizes, *refs):
     n_gz, n_gx = sizes
     ins, outs, land = refs[:8], refs[8:11], refs[11:19]
-    (s_buf, rs_buf, a_buf, q0, q1, result, c_buf, v_a, v_b, u_a, u_b, count, late, in_send, in_recv, c_send, c_recv, o_send,
-     o_recv) = refs[19:]
+    (s_buf, rs_buf, a_buf, q0, q1, result, c_buf, u2, v_a, v_b, u_a, u_b, count, late, in_send, in_recv, c_send, c_recv,
+     o_send, o_recv) = refs[19:]
     g, w, c = lax.axis_index("gz"), lax.axis_index("gx"), lax.axis_index("gy")
     lowest, highest, leftmost, rightmost = g == 0, g == n_gz - 1, w == 0, w == n_gx - 1
 
@@ -262,7 +264,7 @@
                 s_buf[kind, z, t, after, :] = s
         return 0
 
-    lax.fori_loop(0, LAYERS, roots, 0)
+    lax.fori_loop(0, LAYERS, roots, 0, unroll=2)
 
     def stays(z, _):
         for kind in (0, 1):
@@ -271,7 +273,101 @@
                 a_buf[kind, z, t, pl.ds(TOP, SPAN), :] = 1.0 - centre[t] * sums[t]
         return 0
 
-    lax.fori_loop(1, LAYERS - 1, stays, 0)
+    lax.fori_loop(1, LAYERS - 1, stays, 0, unroll=5)
+
+    above_there, below_there = jnp.logical_or(c == 0, jnp.logical_not(highest)), jnp.logical_or(c == 1, jnp.logical_not(lowest))
+    upward, downward = c, c - 1
+
+    def shape(deep, dz, dx):
+        return (deep, NX) if dx == 0 else (deep - 1, deep - 1) if dz != 0 else (OWN, deep)
+
+    def exchange(buf, k, deep, ways, start):
+        for dz, dx in ways:
+            depth, rows = shape(deep, dz, dx)
+            src_z, dst_z = {1: (CHARGE + OWN - depth, CHARGE - depth), -1: (CHARGE, CHARGE + OWN), 0: (CHARGE, CHARGE)}[dz]
+            src_x, dst_x = {1: (FIRST + NX - rows, FIRST - rows), -1: (FIRST, FIRST + NX), 0: (FIRST, FIRST)}[dx]
+            way = 3 * dz + dx + 4
+            chip = {1: upward, -1: downward, 0: 0}[dz]
+            core = c if dz == 0 else 1 - c
+            src = buf.at[pl.ds(src_z, depth), :, pl.ds(src_x, rows), :]
+            dst = buf.at[pl.ds(dst_z, depth), :, pl.ds(dst_x, rows), :]
+
+            def one(src=src, dst=dst, way=way, target=at(chip, dx, core)):
+                copy = pltpu.make_async_remote_copy(
+                    src_ref=src,
+                    dst_ref=dst,
+                    send_sem=c_send.at[k, way],
+                    recv_sem=c_recv.at[k, way],
+                    device_id=target,
+                    device_id_type=MESH,
+                )
+                if start:
+                    copy.start()
+                else:
+                    copy.wait_send()
+
+            when(both({1: above_there, -1: below_there, 0: None}[dz], exists(0, dx)), one)
+
+    def exchanged(buf, k, deep, ways):
+        for dz, dx in ways:
+            depth, rows = shape(deep, dz, dx)
+            view = buf.at[pl.ds(0, depth), :, pl.ds(0, rows), :]
+            way = 3 * dz + dx + 4
+
+            def one(view=view, way=way):
+                pltpu.make_async_copy(view, view, c_recv.at[k, way]).wait()
+
+            when(both({1: below_there, -1: above_there, 0: None}[dz], exists(0, -dx)), one)
+
+    def clear_outside(buf):
+        def clear(condition, start, layers, first, rows):
+            @pl.when(condition)
+            def _():
+                for z in range(start, start + layers):
+                    buf[z, :, pl.ds(first, rows), :] = jnp.zeros((TILES, rows, 128), jnp.float32)
+
+        clear(jnp.logical_not(below_there), 0, CHARGE, 0, ROWS)
+        clear(jnp.logical_not(above_there), CHARGE + OWN, CHARGE, 0, ROWS)
+        clear(leftmost, 0, OWN + 2 * CHARGE, TOP, FIRST - TOP)
+        clear(rightmost, 0, OWN + 2 * CHARGE, FIRST + NX, FIRST - TOP)
+
+    ways = [(1, 1), (-1, 1), (1, -1), (-1, -1), (0, 1), (0, -1), (1, 0), (-1, 0)]
+    arrived(POTENTIAL)
+
+    def spread(z, _):
+        in_z = layer_in(z, EARLY).astype(jnp.int32)
+        own_mask, halo_mask = jnp.broadcast_to(in_z, (NX, 128)) > 0, halo_inside * in_z > 0
+        for t in range(TILES):
+            tile = pl.ds(128 * t, 128)
+            u_a[z, t, own, :] = jnp.where(own_mask, land[PHI][z, pl.ds(0, NX), tile], 0.0)
+            phi = jnp.where(halo_mask, land[PHI][z, halo, tile], 0.0)
+            u_a[z, t, before, :] = phi
+            u_a[z, t, after, :] = phi
+        return 0
+
+    lax.fori_loop(0, OWN + 2 * EARLY, spread, 0, unroll=2)
+
+    span = pl.ds(TOP, SPAN)
+
+    def first_sweep(z, _):
+        _, sums = around(u_a, z, TOP, SPAN)
+        weight = jnp.where(splat(layer_in(z, EARLY), SPAN), sixth, 0.0)
+        for t in range(TILES):
+            u_b[z, t, span, :] = sums[t] * weight
+        return 0
+
+    lax.fori_loop(1, OWN + 2 * EARLY - 1, first_sweep, 0, unroll=5)
+
+    def second_sweep(z, _):
+        _, sums = around(u_b, z + EARLY, FIRST, NX)
+        for t in range(TILES):
+            u2[z + CHARGE, t, own, :] = sums[t] * (1.0 / 6.0)
+        return 0
+
+    lax.fori_loop(0, OWN, second_sweep, 0, unroll=4)
+    exchange(u2, 1, EARLY, ways, True)
+    clear_outside(u2)
+    clear_outside(c_buf)
 
     arrived(DENSITIES)
     for from_row, to_row in ((0, 8), (8, 16), (16, 24)):
@@ -306,8 +402,6 @@
 
         lax.fori_loop(0, TILES, drift, 0)
 
-    span = pl.ds(TOP, SPAN)
-
     def sweep_one(z, _):
         for kind in (0, 1):
             centre, sums = around(q0.at[kind], z, TOP, SPAN)
@@ -316,7 +410,7 @@
                 q1[kind, z, t, span, :] = centre[t] * a_buf[kind, z, t, span, :] + (s * s) * sums[t]
         return 0
 
-    lax.fori_loop(1, LAYERS - 1, sweep_one, 0)
+    lax.fori_loop(1, LAYERS - 1, sweep_one, 0, unroll=5)
 
     arrived(DOPING)
 
@@ -336,49 +430,9 @@
             c_buf[z + CHARGE, t, own, :] = (found[1][t] - found[0][t] + doping) * (0.5 / 6.0)
         return 0
 
-    lax.fori_loop(0, OWN, sweep_two, 0)
-
-    above_there, below_there = jnp.logical_or(c == 0, jnp.logical_not(highest)), jnp.logical_or(c == 1, jnp.logical_not(lowest))
-    upward, downward = c, c - 1
-
-    def exchange(ways, start):
-        for dz, dx in ways:
-            depth, rows = (CHARGE, NX) if dx == 0 else (CHARGE - 1, CHARGE - 1) if dz != 0 else (OWN, CHARGE)
-            src_z, dst_z = {1: (CHARGE + OWN - depth, CHARGE - depth), -1: (CHARGE, CHARGE + OWN), 0: (CHARGE, CHARGE)}[dz]
-            src_x, dst_x = {1: (FIRST + NX - rows, FIRST - rows), -1: (FIRST, FIRST + NX), 0: (FIRST, FIRST)}[dx]
-            way = 3 * dz + dx + 4
-            chip = {1: upward, -1: downward, 0: 0}[dz]
-            core = c if dz == 0 else 1 - c
-
-            def one(src_z=src_z, dst_z=dst_z, src_x=src_x, dst_x=dst_x, depth=depth, rows=rows, way=way, chip=chip, core=core, dx=dx):
-                copy = pltpu.make_async_remote_copy(
-                    src_ref=c_buf.at[pl.ds(src_z, depth), :, pl.ds(src_x, rows), :],
-                    dst_ref=c_buf.at[pl.ds(dst_z, depth), :, pl.ds(dst_x, rows), :],
-                    send_sem=c_send.at[way],
-                    recv_sem=c_recv.at[way],
-                    device_id=at(chip, dx, core),
-                    device_id_type=MESH,
-                )
-                if start:
-                    copy.start()
-                else:
-                    copy.wait_send()
-
-            when(both({1: above_there, -1: below_there, 0: None}[dz], exists(0, dx)), one)
-
-    def charge_arrived(ways):
-        for dz, dx in ways:
-            depth, rows = (CHARGE, NX) if dx == 0 else (CHARGE - 1, CHARGE - 1) if dz != 0 else (OWN, CHARGE)
-            view = c_buf.at[pl.ds(0, depth), :, pl.ds(0, rows), :]
-            way = 3 * dz + dx + 4
-
-            def one(view=view, way=way):
-                pltpu.make_async_copy(view, view, c_recv.at[way]).wait()
-
-            when(both({1: below_there, -1: above_there, 0: None}[dz], exists(0, -dx)), one)
-
-    ways = [(1, 1), (-1, 1), (1, -1), (-1, -1), (0, 1), (0, -1), (1, 0), (-1, 0)]
-    exchange(ways, True)
+    lax.fori_loop(0, OWN, sweep_two, 0, unroll=4)
+
+    exchange(c_buf, 0, CHARGE, ways, True)
 
     mine = pl.ds(pl.multiple_of(c * OWN, OWN), OWN)
 
@@ -398,71 +452,36 @@
     give(0)
     give(1)
 
-    arrived(POTENTIAL)
-
-    def spread(z, _):
-        in_z = layer_in(z, SWEEPS).astype(jnp.int32)
-        own_mask, halo_mask = jnp.broadcast_to(in_z, (NX, 128)) > 0, halo_inside * in_z > 0
-        for t in range(TILES):
-            tile = pl.ds(128 * t, 128)
-            u_a[z, t, own, :] = jnp.where(own_mask, land[PHI][z, pl.ds(0, NX), tile], 0.0)
-            phi = jnp.where(halo_mask, land[PHI][z, halo, tile], 0.0)
-            u_a[z, t, before, :] = phi
-            u_a[z, t, after, :] = phi
-        return 0
-
-    lax.fori_loop(0, OWN + 2 * SWEEPS, spread, 0)
-
-    def sweep(src, dst, below, start, stop, charge=None):
+    exchanged(c_buf, 0, CHARGE, ways)
+    exchanged(u2, 1, EARLY, ways)
+
+    def sweep(src, dst, start, stop, unroll, *more):
         def body(z, _):
             _, sums = around(src, z, TOP, SPAN)
-            weight = jnp.where(splat(layer_in(z, below), SPAN), sixth, 0.0)
+            weight = jnp.where(splat(layer_in(z, CHARGE), SPAN), sixth, 0.0)
             for t in range(TILES):
-                value = sums[t] * weight
-                if charge is not None:
-                    value = value + charge[z, t, span, :]
+                value = sums[t] * weight + c_buf[z, t, span, :]
+                for ref in more:
+                    value = value + ref[z, t, span, :]
                 dst[z, t, span, :] = value
             return 0
 
-        lax.fori_loop(start, stop, body, 0, unroll=2)
-
-    sweep(u_a, u_b, SWEEPS, 1, OWN + 2 * SWEEPS - 1)
-    sweep(u_b, u_a, SWEEPS, 2, OWN + 2 * SWEEPS - 2)
-    sweep(u_a, u_b, SWEEPS, 3, OWN + 2 * SWEEPS - 3)
-
-    def sweep_four(z, _):
-        _, sums = around(u_b, z + SWEEPS, FIRST, NX)
-        for t in range(TILES):
-            u_a[z, t, own, :] = sums[t] * (1.0 / 6.0)
-        return 0
-
-    lax.fori_loop(0, OWN, sweep_four, 0, unroll=2)
-
-    def clear(condition, start, layers, first, rows):
-        @pl.when(condition)
-        def _():
-            for z in range(start, start + layers):
-                c_buf[z, :, pl.ds(first, rows), :] = jnp.zeros((TILES, rows, 128), jnp.float32)
-
-    clear(jnp.logical_not(below_there), 0, CHARGE, 0, ROWS)
-    clear(jnp.logical_not(above_there), CHARGE + OWN, CHARGE, 0, ROWS)
-    clear(leftmost, 0, OWN + 2 * CHARGE, TOP, FIRST - TOP)
-    clear(rightmost, 0, OWN + 2 * CHARGE, FIRST + NX, FIRST - TOP)
-    charge_arrived(ways)
-
-    sweep(c_buf, v_a, CHARGE, 1, OWN + 2 * CHARGE - 1, c_buf)
-    sweep(v_a, v_b, CHARGE, 2, OWN + 2 * CHARGE - 2, c_buf)
+        lax.fori_loop(start, stop, body, 0, unroll=unroll)
+
+    sweep(c_buf, v_a, 1, OWN + 2 * CHARGE - 1, 6, u2)
+    sweep(v_a, v_b, 2, OWN + 2 * CHARGE - 2, 5)
 
     def last_sweep(z, _):
         _, sums = around(v_b, z + CHARGE, FIRST, NX)
         for t in range(TILES):
-            result[2, z, t, own, :] = (sums[t] * (1.0 / 6.0) + c_buf[z + CHARGE, t, own, :]) + u_a[z, t, own, :]
-        return 0
-
-    lax.fori_loop(0, OWN, last_sweep, 0, unroll=2)
+            result[2, z, t, own, :] = sums[t] * (1.0 / 6.0) + c_buf[z + CHARGE, t, own, :]
+        return 0
+
+    lax.fori_loop(0, OWN, last_sweep, 0, unroll=8)
     give(2)
 
-    exchange(ways, False)
+    exchange(c_buf, 0, CHARGE, ways, False)
+    exchange(u2, 1, EARLY, ways, False)
     for dz, dx in SIDES:
         when(exists(dz, dx), lambda dz=dz, dx=dx: wait_rows(sent((dz, dx)), in_send.at[3 * dz + dx + 4]))
     for index in range(3):
@@ -511,14 +530,15 @@
             work(OWN + 2 * CHARGE),
             work(OWN + 2 * CHARGE),
             work(OWN + 2 * CHARGE),
-            work(OWN + 2 * SWEEPS),
-            work(OWN + 2 * SWEEPS),
+            work(OWN + 2 * CHARGE),
+            work(OWN + 2 * EARLY),
+            work(OWN + 2 * EARLY),
             pltpu.VMEM((most, 128), jnp.float32),
             pltpu.SemaphoreType.REGULAR,
             dma((9,)),
             dma((4, 9)),
-            dma((9,)),
-            dma((9,)),
+            dma((2, 9)),
+            dma((2, 9)),
             dma((3, 4)),
             dma((3, 2)),
         ],

time: 36.9 us -> 34.2 us (0.927)
  Pallas kernels: 36.1 us -> 33.4 us
    pallas_call x1, Pallas kernels: 35.2 us -> 32.5 us  [on_device(): pl.pallas_call(lambda *refs: kernel(sizes, *refs), out_shape=[pltpu.VMEM(...]
where the time goes in v3:
time: 34.2 us; the launch traced here: 34.1 us
  Pallas kernels  33.4 us (98%)
  between operations  0.64 us (2%)
    pallas_call x1, Pallas kernels, on_device(): pl.pallas_call(lambda *refs: kernel(sizes, *refs), out_shape=[pltpu.VMEM(...  32.5 us
    pallas_call x1, Pallas kernels, on_device(): pl.pallas_call(hand_over, out_shape=shapes, in_specs=[pl.BlockSpec(memory...  0.9 us

profile of v3, /device:TPU:31, one launch (start us, length us, event | category | flops | bytes accessed | tf_op | source)
XLA Modules:
  0.0 34.1 jit_solution(14044543039852307473)
XLA Ops:
  0.6 32.5 %shard_map.103 = (f32[16,16,256]{2,1,0:T(8,128)S(1)}, f32[16,16,256]{2,1,0:T(8,128)S(1)}, f32[16,16,256]{2,1,0:T(8,128)S(1)}) custom-call(f32[16,16,256]{2,1,0:T(8,128)} %refs_0_.1, f32[16,16,256]{2,1,0:T(8,128)} %refs_1_.1, f32[16,16,256]{2,1,0:T(8,128)} %refs_2_.1, f32[16,16,256]{2,1,0:T(8,128)} %refs_3_.1, f32[16,16,256]{2,1,0:T(8,128)} %refs_4_.1, ...), custom_call_target="tpu_custom_call" | custom-call | tf_op jit(solution)/shard_map/pallas_call | solution.py:517
  33.2 0.9 %shard_map.104 = (f32[16,16,256]{2,1,0:T(8,128)}, f32[16,16,256]{2,1,0:T(8,128)}, f32[16,16,256]{2,1,0:T(8,128)}) custom-call(f32[16,16,256]{2,1,0:T(8,128)S(1)} %get-tuple-element.6.refs_0_, f32[16,16,256]{2,1,0:T(8,128)S(1)} %get-tuple-element.7.refs_1_, f32[16,16,256]{2,1,0:T(8,128)S(1)} %get-tuple-element.8.refs_2_), custom_call_target="tpu_custom_call" | custom-call | tf_op jit(solution)/shard_map/pallas_call | solution.py:547

commit v4 on v3

--- a/solution.py
+++ b/solution.py
@@ -20,20 +20,20 @@
 CHARGE = 3
 EARLY = 2
 DIFFUSION = 2
-UP = CFL_MAX + 1 + DIFFUSION
+UP = CFL_MAX + 1
 LAYERS = OWN + 2 * DIFFUSION
 SEAM = 8
 
 E, H, ME, MH, PHI, DOP, CFL, FRAC = range(8)
 REACH = {
-    E: (DIFFUSION, UP, DIFFUSION),
-    H: (DIFFUSION, DIFFUSION, UP),
+    E: (0, UP, 0),
+    H: (0, 0, UP),
     ME: (DIFFUSION, DIFFUSION, DIFFUSION),
     MH: (DIFFUSION, DIFFUSION, DIFFUSION),
     PHI: (EARLY, EARLY, EARLY),
     DOP: (0, 0, 0),
-    CFL: (DIFFUSION, 0, 0),
-    FRAC: (DIFFUSION, 0, 0),
+    CFL: (0, 0, 0),
+    FRAC: (0, 0, 0),
 }
 FLAT = (CFL, FRAC)
 GROUPS = ((ME, MH), (PHI,), (E, H, CFL, FRAC), (DOP,))
@@ -169,8 +169,8 @@
         view = count.at[pl.ds(0, rows), :]
         pltpu.make_async_copy(view, view, sem).wait()
 
-    def arrived(group):
-        for dz, dx in SIDES:
+    def arrived(group, sides=SIDES):
+        for dz, dx in sides:
             for core in (0, 1):
                 rows = received(group, core, (dz, dx))
                 if rows == 0:
@@ -185,16 +185,14 @@
     right = [(dz, 1) for dz in (1, -1, 0)]
     left = [(dz, -1) for dz in (1, -1, 0)]
     near = [(1, 0), (-1, 0), (0, 0)]
-    for group in range(4):
+    push_all(DENSITIES, near)
+    push_all(MOBILITIES, [(0, 0)])
+    for group in (MOBILITIES, POTENTIAL):
         push_all(group, right)
         push_all(group, left, jnp.logical_not(seam_left))
-        push_all(group, near)
-
-    @pl.when(seam_left)
-    def _():
-        pl.semaphore_wait(late, 2 * deep)
-        for group in range(4):
-            push_all(group, left)
+        push_all(group, near[:2])
+    push_all(POTENTIAL, [(0, 0)])
+    push_all(DOPING, [(0, 0)])
 
     def splat(flag, rows):
         return jnp.broadcast_to(flag.astype(jnp.int32), (rows, 128)) > 0
@@ -229,68 +227,36 @@
 
     def empty(field, start, layers):
         for z in range(start, start + layers):
-            land[field][z] = jnp.zeros((LANDING, 2 * NL), jnp.float32)
+            land[field][z] = jnp.zeros((NX, 2 * NL), jnp.float32)
 
     for core in (0, 1):
 
         @pl.when(jnp.logical_and(lowest, c == core))
         def _(core=core):
             empty(E, 0, UP - OWN * core)
-            if core == 0:
-                empty(H, 0, DIFFUSION)
 
         @pl.when(jnp.logical_and(highest, c == core))
         def _(core=core):
-            empty(H, DIFFUSION + NZ - OWN * core, UP - OWN * (1 - core))
-            if core == 1:
-                empty(E, UP + OWN, DIFFUSION)
-
-    arrived(MOBILITIES)
+            empty(H, NZ - OWN * core, UP - OWN * (1 - core))
+
     own, halo = pl.ds(FIRST, NX), pl.ds(NX, 8)
     after, before = pl.ds(FIRST + NX, 8), pl.ds(0, 8)
-
-    def roots(z, _):
-        in_z = layer_in(z, DIFFUSION).astype(jnp.int32)
-        own_mask, halo_mask = jnp.broadcast_to(in_z, (NX, 128)) > 0, halo_inside * in_z > 0
-        for kind, field in ((0, ME), (1, MH)):
-            for t in range(TILES):
-                m = land[field][z, pl.ds(0, NX), pl.ds(128 * t, 128)]
-                rs = lax.rsqrt(m)
-                rs_buf[kind, z, t] = rs
-                s_buf[kind, z, t, own, :] = jnp.where(own_mask, m * rs, 0.0)
-                m = land[field][z, halo, pl.ds(128 * t, 128)]
-                s = jnp.where(halo_mask, m * lax.rsqrt(m), 0.0)
-                s_buf[kind, z, t, before, :] = s
-                s_buf[kind, z, t, after, :] = s
-        return 0
-
-    lax.fori_loop(0, LAYERS, roots, 0, unroll=2)
-
-    def stays(z, _):
-        for kind in (0, 1):
-            centre, sums = around(s_buf.at[kind], z, TOP, SPAN)
-            for t in range(TILES):
-                a_buf[kind, z, t, pl.ds(TOP, SPAN), :] = 1.0 - centre[t] * sums[t]
-        return 0
-
-    lax.fori_loop(1, LAYERS - 1, stays, 0, unroll=5)
-
     above_there, below_there = jnp.logical_or(c == 0, jnp.logical_not(highest)), jnp.logical_or(c == 1, jnp.logical_not(lowest))
     upward, downward = c, c - 1
 
     def shape(deep, dz, dx):
         return (deep, NX) if dx == 0 else (deep - 1, deep - 1) if dz != 0 else (OWN, deep)
 
-    def exchange(buf, k, deep, ways, start):
+    def exchange(buf, k, deep, ways, start, base=CHARGE, lead=()):
         for dz, dx in ways:
             depth, rows = shape(deep, dz, dx)
-            src_z, dst_z = {1: (CHARGE + OWN - depth, CHARGE - depth), -1: (CHARGE, CHARGE + OWN), 0: (CHARGE, CHARGE)}[dz]
+            src_z, dst_z = {1: (base + OWN - depth, base - depth), -1: (base, base + OWN), 0: (base, base)}[dz]
             src_x, dst_x = {1: (FIRST + NX - rows, FIRST - rows), -1: (FIRST, FIRST + NX), 0: (FIRST, FIRST)}[dx]
             way = 3 * dz + dx + 4
             chip = {1: upward, -1: downward, 0: 0}[dz]
             core = c if dz == 0 else 1 - c
-            src = buf.at[pl.ds(src_z, depth), :, pl.ds(src_x, rows), :]
-            dst = buf.at[pl.ds(dst_z, depth), :, pl.ds(dst_x, rows), :]
+            src = buf.at[*lead, pl.ds(src_z, depth), :, pl.ds(src_x, rows), :]
+            dst = buf.at[*lead, pl.ds(dst_z, depth), :, pl.ds(dst_x, rows), :]
 
             def one(src=src, dst=dst, way=way, target=at(chip, dx, core)):
                 copy = pltpu.make_async_remote_copy(
@@ -308,10 +274,10 @@
 
             when(both({1: above_there, -1: below_there, 0: None}[dz], exists(0, dx)), one)
 
-    def exchanged(buf, k, deep, ways):
+    def exchanged(buf, k, deep, ways, lead=()):
         for dz, dx in ways:
             depth, rows = shape(deep, dz, dx)
-            view = buf.at[pl.ds(0, depth), :, pl.ds(0, rows), :]
+            view = buf.at[*lead, pl.ds(0, depth), :, pl.ds(0, rows), :]
             way = 3 * dz + dx + 4
 
             def one(view=view, way=way):
@@ -319,19 +285,103 @@
 
             when(both({1: below_there, -1: above_there, 0: None}[dz], exists(0, -dx)), one)
 
-    def clear_outside(buf):
+    def clear_outside(buf, halo):
         def clear(condition, start, layers, first, rows):
             @pl.when(condition)
             def _():
                 for z in range(start, start + layers):
                     buf[z, :, pl.ds(first, rows), :] = jnp.zeros((TILES, rows, 128), jnp.float32)
 
-        clear(jnp.logical_not(below_there), 0, CHARGE, 0, ROWS)
-        clear(jnp.logical_not(above_there), CHARGE + OWN, CHARGE, 0, ROWS)
-        clear(leftmost, 0, OWN + 2 * CHARGE, TOP, FIRST - TOP)
-        clear(rightmost, 0, OWN + 2 * CHARGE, FIRST + NX, FIRST - TOP)
+        clear(jnp.logical_not(below_there), 0, halo, 0, ROWS)
+        clear(jnp.logical_not(above_there), halo + OWN, halo, 0, ROWS)
+        clear(leftmost, 0, OWN + 2 * halo, TOP, FIRST - TOP)
+        clear(rightmost, 0, OWN + 2 * halo, FIRST + NX, FIRST - TOP)
 
     ways = [(1, 1), (-1, 1), (1, -1), (-1, -1), (0, 1), (0, -1), (1, 0), (-1, 0)]
+    for kind in (0, 1):
+        clear_outside(q0.at[kind], DIFFUSION)
+    clear_outside(u2, CHARGE)
+    clear_outside(c_buf, CHARGE)
+
+    arrived(MOBILITIES, [(0, 0)])
+
+    def own_roots(z, there):
+        mask = None if there is None else jnp.broadcast_to(there, (NX, 128)) > 0
+        for kind, field in ((0, ME), (1, MH)):
+            for t in range(TILES):
+                m = land[field][z, pl.ds(0, NX), pl.ds(128 * t, 128)]
+                rs = lax.rsqrt(m)
+                rs_buf[kind, z, t] = rs
+                s_buf[kind, z, t, own, :] = m * rs if mask is None else jnp.where(mask, m * rs, 0.0)
+
+    def roots(z, _):
+        own_roots(z, None)
+        return 0
+
+    lax.fori_loop(DIFFUSION, DIFFUSION + OWN, roots, 0, unroll=4)
+
+    arrived(DENSITIES)
+    for half in (0, 1):
+        rows, target = pl.ds(8 * half, 8), pl.ds(FIRST + 8 * half, 8)
+
+        def drift(t, _, rows=rows, target=target):
+            tile = pl.ds(pl.multiple_of(t * 128, 128), 128)
+            d = land[CFL][rows, tile]
+            f = land[FRAC][rows, tile]
+            rest = 1.0 - f
+            bits = [(k, jnp.bitwise_and(d, k) != 0) for k in (8, 4, 2, 1)]
+            for kind, field in ((0, E), (1, H)):
+                length = OWN + UP
+                if kind == 0:
+                    v = [land[field][length - 1 - i, rows, tile] for i in range(length)]
+                else:
+                    v = [land[field][i, rows, tile] for i in range(length)]
+                for k, bit in bits:
+                    if k == 8:
+                        v = [jnp.where(bit, v[i + 8], v[i]) if i <= OWN else v[i] for i in range(length - 1)]
+                    else:
+                        v = [jnp.where(bit, v[i + k], v[i]) for i in range(len(v) - k)]
+                for i in range(OWN):
+                    z = DIFFUSION + (OWN - 1 - i if kind == 0 else i)
+                    q0[kind, z, t, target, :] = (rest * v[i] + f * v[i + 1]) * s_buf[kind, z, t, target, :]
+            return 0
+
+        lax.fori_loop(0, TILES, drift, 0, unroll=2)
+
+    @pl.when(seam_left)
+    def _():
+        pl.semaphore_wait(late, 2 * deep)
+        for group in (MOBILITIES, POTENTIAL):
+            push_all(group, left)
+
+    kinds = (slice(None),)
+    exchange(q0, 2, DIFFUSION, ways, True, DIFFUSION, kinds)
+
+    arrived(MOBILITIES, SIDES[:-1])
+    for z in (*range(DIFFUSION), *range(DIFFUSION + OWN, LAYERS)):
+        own_roots(z, layer_in(z, DIFFUSION).astype(jnp.int32))
+
+    def halo_roots(z, _):
+        mask = halo_inside * layer_in(z, DIFFUSION).astype(jnp.int32) > 0
+        for kind, field in ((0, ME), (1, MH)):
+            for t in range(TILES):
+                m = land[field][z, halo, pl.ds(128 * t, 128)]
+                s = jnp.where(mask, m * lax.rsqrt(m), 0.0)
+                s_buf[kind, z, t, before, :] = s
+                s_buf[kind, z, t, after, :] = s
+        return 0
+
+    lax.fori_loop(0, LAYERS, halo_roots, 0, unroll=4)
+
+    def stays(z, _):
+        for kind in (0, 1):
+            centre, sums = around(s_buf.at[kind], z, TOP, SPAN)
+            for t in range(TILES):
+                a_buf[kind, z, t, pl.ds(TOP, SPAN), :] = 1.0 - centre[t] * sums[t]
+        return 0
+
+    lax.fori_loop(1, LAYERS - 1, stays, 0, unroll=5)
+
     arrived(POTENTIAL)
 
     def spread(z, _):
@@ -366,42 +416,8 @@
 
     lax.fori_loop(0, OWN, second_sweep, 0, unroll=4)
     exchange(u2, 1, EARLY, ways, True)
-    clear_outside(u2)
-    clear_outside(c_buf)
-
-    arrived(DENSITIES)
-    for from_row, to_row in ((0, 8), (8, 16), (16, 24)):
-        rows, target = pl.ds(from_row, 8), pl.ds(to_row, 8)
-
-        def drift(t, _, rows=rows, target=target, at_halo=from_row == NX):
-            tile = pl.ds(pl.multiple_of(t * 128, 128), 128)
-            d = land[CFL][rows, tile]
-            f = land[FRAC][rows, tile]
-            rest = 1.0 - f
-            bits = [(k, jnp.bitwise_and(d, k) != 0) for k in (8, 4, 2, 1)]
-            mask = halo_inside > 0
-            for kind, field in ((0, E), (1, H)):
-                length = LAYERS + CFL_MAX + 1
-                if kind == 0:
-                    v = [land[field][length - 1 - i, rows, tile] for i in range(length)]
-                else:
-                    v = [land[field][i, rows, tile] for i in range(length)]
-                for k, bit in bits:
-                    if k == 8:
-                        v = [jnp.where(bit, v[i + 8], v[i]) if i <= LAYERS else v[i] for i in range(length - 1)]
-                    else:
-                        v = [jnp.where(bit, v[i + k], v[i]) for i in range(len(v) - k)]
-                for i in range(LAYERS):
-                    z = LAYERS - 1 - i if kind == 0 else i
-                    q = (rest * v[i] + f * v[i + 1]) * s_buf[kind, z, t, target, :]
-                    if at_halo:
-                        q = jnp.where(mask, q, 0.0)
-                        q0[kind, z, t, before, :] = q
-                    q0[kind, z, t, target, :] = q
-            return 0
-
-        lax.fori_loop(0, TILES, drift, 0)
-
+
+    exchanged(q0, 2, DIFFUSION, ways, kinds)
     def sweep_one(z, _):
         for kind in (0, 1):
             centre, sums = around(q0.at[kind], z, TOP, SPAN)
@@ -482,6 +498,7 @@
 
     exchange(c_buf, 0, CHARGE, ways, False)
     exchange(u2, 1, EARLY, ways, False)
+    exchange(q0, 2, DIFFUSION, ways, False, DIFFUSION, kinds)
     for dz, dx in SIDES:
         when(exists(dz, dx), lambda dz=dz, dx=dx: wait_rows(sent((dz, dx)), in_send.at[3 * dz + dx + 4]))
     for index in range(3):
@@ -537,8 +554,8 @@
             pltpu.SemaphoreType.REGULAR,
             dma((9,)),
             dma((4, 9)),
-            dma((2, 9)),
-            dma((2, 9)),
+            dma((3, 9)),
+            dma((3, 9)),
             dma((3, 4)),
             dma((3, 2)),
         ],

time: 34.2 us -> 32.7 us (0.956)
  Pallas kernels: 33.4 us -> 31.9 us
    pallas_call x1, Pallas kernels: 32.5 us -> 31 us  [on_device(): pl.pallas_call(lambda *refs: kernel(sizes, *refs), out_shape=[pltpu.VMEM(...]
where the time goes in v4:
time: 32.7 us; the launch traced here: 32.6 us
  Pallas kernels  31.9 us (98%)
  between operations  0.64 us (2%)
    pallas_call x1, Pallas kernels, on_device(): pl.pallas_call(lambda *refs: kernel(sizes, *refs), out_shape=[pltpu.VMEM(...  31 us
    pallas_call x1, Pallas kernels, on_device(): pl.pallas_call(hand_over, out_shape=shapes, in_specs=[pl.BlockSpec(memory...  0.9 us

profile of v4, /device:TPU:31, one launch (start us, length us, event | category | flops | bytes accessed | tf_op | source)
XLA Modules:
  0.0 32.6 jit_solution(12624769203261966829)
XLA Ops:
  0.6 31.0 %shard_map.103 = (f32[16,16,256]{2,1,0:T(8,128)S(1)}, f32[16,16,256]{2,1,0:T(8,128)S(1)}, f32[16,16,256]{2,1,0:T(8,128)S(1)}) custom-call(f32[16,16,256]{2,1,0:T(8,128)} %refs_0_.1, f32[16,16,256]{2,1,0:T(8,128)} %refs_1_.1, f32[16,16,256]{2,1,0:T(8,128)} %refs_2_.1, f32[16,16,256]{2,1,0:T(8,128)} %refs_3_.1, f32[16,16,256]{2,1,0:T(8,128)} %refs_4_.1, ...), custom_call_target="tpu_custom_call" | custom-call | tf_op jit(solution)/shard_map/pallas_call | solution.py:534
  31.7 0.9 %shard_map.104 = (f32[16,16,256]{2,1,0:T(8,128)}, f32[16,16,256]{2,1,0:T(8,128)}, f32[16,16,256]{2,1,0:T(8,128)}) custom-call(f32[16,16,256]{2,1,0:T(8,128)S(1)} %get-tuple-element.6.refs_0_, f32[16,16,256]{2,1,0:T(8,128)S(1)} %get-tuple-element.7.refs_1_, f32[16,16,256]{2,1,0:T(8,128)S(1)} %get-tuple-element.8.refs_2_), custom_call_target="tpu_custom_call" | custom-call | tf_op jit(solution)/shard_map/pallas_call | solution.py:564

commit v5 on v4

--- a/solution.py
+++ b/solution.py
@@ -297,7 +297,9 @@
         clear(leftmost, 0, OWN + 2 * halo, TOP, FIRST - TOP)
         clear(rightmost, 0, OWN + 2 * halo, FIRST + NX, FIRST - TOP)
 
-    ways = [(1, 1), (-1, 1), (1, -1), (-1, -1), (0, 1), (0, -1), (1, 0), (-1, 0)]
+    to_right = [(1, 1), (-1, 1), (0, 1)]
+    to_others = [(1, -1), (-1, -1), (0, -1), (1, 0), (-1, 0)]
+    ways = to_right + to_others
     for kind in (0, 1):
         clear_outside(q0.at[kind], DIFFUSION)
     clear_outside(u2, CHARGE)
@@ -321,7 +323,8 @@
     lax.fori_loop(DIFFUSION, DIFFUSION + OWN, roots, 0, unroll=4)
 
     arrived(DENSITIES)
-    for half in (0, 1):
+    kinds = (slice(None),)
+    for half in (1, 0):
         rows, target = pl.ds(8 * half, 8), pl.ds(FIRST + 8 * half, 8)
 
         def drift(t, _, rows=rows, target=target):
@@ -347,6 +350,8 @@
             return 0
 
         lax.fori_loop(0, TILES, drift, 0, unroll=2)
+        if half == 1:
+            exchange(q0, 2, DIFFUSION, to_right, True, DIFFUSION, kinds)
 
     @pl.when(seam_left)
     def _():
@@ -354,33 +359,7 @@
         for group in (MOBILITIES, POTENTIAL):
             push_all(group, left)
 
-    kinds = (slice(None),)
-    exchange(q0, 2, DIFFUSION, ways, True, DIFFUSION, kinds)
-
-    arrived(MOBILITIES, SIDES[:-1])
-    for z in (*range(DIFFUSION), *range(DIFFUSION + OWN, LAYERS)):
-        own_roots(z, layer_in(z, DIFFUSION).astype(jnp.int32))
-
-    def halo_roots(z, _):
-        mask = halo_inside * layer_in(z, DIFFUSION).astype(jnp.int32) > 0
-        for kind, field in ((0, ME), (1, MH)):
-            for t in range(TILES):
-                m = land[field][z, halo, pl.ds(128 * t, 128)]
-                s = jnp.where(mask, m * lax.rsqrt(m), 0.0)
-                s_buf[kind, z, t, before, :] = s
-                s_buf[kind, z, t, after, :] = s
-        return 0
-
-    lax.fori_loop(0, LAYERS, halo_roots, 0, unroll=4)
-
-    def stays(z, _):
-        for kind in (0, 1):
-            centre, sums = around(s_buf.at[kind], z, TOP, SPAN)
-            for t in range(TILES):
-                a_buf[kind, z, t, pl.ds(TOP, SPAN), :] = 1.0 - centre[t] * sums[t]
-        return 0
-
-    lax.fori_loop(1, LAYERS - 1, stays, 0, unroll=5)
+    exchange(q0, 2, DIFFUSION, to_others, True, DIFFUSION, kinds)
 
     arrived(POTENTIAL)
 
@@ -417,6 +396,31 @@
     lax.fori_loop(0, OWN, second_sweep, 0, unroll=4)
     exchange(u2, 1, EARLY, ways, True)
 
+    arrived(MOBILITIES, SIDES[:-1])
+    for z in (*range(DIFFUSION), *range(DIFFUSION + OWN, LAYERS)):
+        own_roots(z, layer_in(z, DIFFUSION).astype(jnp.int32))
+
+    def halo_roots(z, _):
+        mask = halo_inside * layer_in(z, DIFFUSION).astype(jnp.int32) > 0
+        for kind, field in ((0, ME), (1, MH)):
+            for t in range(TILES):
+                m = land[field][z, halo, pl.ds(128 * t, 128)]
+                s = jnp.where(mask, m * lax.rsqrt(m), 0.0)
+                s_buf[kind, z, t, before, :] = s
+                s_buf[kind, z, t, after, :] = s
+        return 0
+
+    lax.fori_loop(0, LAYERS, halo_roots, 0, unroll=4)
+
+    def stays(z, _):
+        for kind in (0, 1):
+            centre, sums = around(s_buf.at[kind], z, TOP, SPAN)
+            for t in range(TILES):
+                a_buf[kind, z, t, pl.ds(TOP, SPAN), :] = 1.0 - centre[t] * sums[t]
+        return 0
+
+    lax.fori_loop(1, LAYERS - 1, stays, 0, unroll=5)
+
     exchanged(q0, 2, DIFFUSION, ways, kinds)
     def sweep_one(z, _):
         for kind in (0, 1):
@@ -430,40 +434,41 @@
 
     arrived(DOPING)
 
-    def sweep_two(z, _):
-        found = []
-        for kind in (0, 1):
-            centre, sums = around(q1.at[kind], z + DIFFUSION, FIRST, NX)
-            n = []
+    for half in (1, 0):
+        part = pl.ds(FIRST + 8 * half, 8)
+
+        def sweep_two(z, _, half=half, part=part):
+            found = []
+            for kind in (0, 1):
+                centre, sums = around(q1.at[kind], z + DIFFUSION, FIRST + 8 * half, 8)
+                n = []
+                for t in range(TILES):
+                    s = s_buf[kind, z + DIFFUSION, t, part, :]
+                    q = centre[t] * a_buf[kind, z + DIFFUSION, t, part, :] + (s * s) * sums[t]
+                    n.append(q * rs_buf[kind, z + DIFFUSION, t, pl.ds(8 * half, 8), :])
+                    result[kind, z, t, part, :] = n[t]
+                found.append(n)
             for t in range(TILES):
-                s = s_buf[kind, z + DIFFUSION, t, own, :]
-                q = centre[t] * a_buf[kind, z + DIFFUSION, t, own, :] + (s * s) * sums[t]
-                n.append(q * rs_buf[kind, z + DIFFUSION, t])
-                result[kind, z, t, own, :] = n[t]
-            found.append(n)
-        for t in range(TILES):
-            doping = land[DOP][z, pl.ds(0, NX), pl.ds(128 * t, 128)]
-            c_buf[z + CHARGE, t, own, :] = (found[1][t] - found[0][t] + doping) * (0.5 / 6.0)
-        return 0
-
-    lax.fori_loop(0, OWN, sweep_two, 0, unroll=4)
-
-    exchange(c_buf, 0, CHARGE, ways, True)
-
-    mine = pl.ds(pl.multiple_of(c * OWN, OWN), OWN)
-
-    def give(index):
+                doping = land[DOP][z, pl.ds(8 * half, 8), pl.ds(128 * t, 128)]
+                c_buf[z + CHARGE, t, part, :] = (found[1][t] - found[0][t] + doping) * (0.5 / 6.0)
+            return 0
+
+        lax.fori_loop(0, OWN, sweep_two, 0, unroll=8)
+        exchange(c_buf, 0, CHARGE, to_right if half == 1 else to_others, True)
+
+    def give(index, first=0, layers=OWN):
+        mine, part = pl.ds(c * OWN + first, layers), pl.ds(first, layers)
         for k in range(TILES // 2):
             there = outs[index].at[mine, :, pl.ds(128 * k, 128)]
             pltpu.make_async_remote_copy(
-                src_ref=result.at[index, :, 2 * (1 - c) + k, pl.ds(FIRST, NX), :],
+                src_ref=result.at[index, part, 2 * (1 - c) + k, pl.ds(FIRST, NX), :],
                 dst_ref=there,
                 send_sem=o_send.at[index, k],
                 recv_sem=o_recv.at[index, k],
                 device_id=at(0, 0, 1 - c),
                 device_id_type=MESH,
             ).start()
-            pltpu.make_async_copy(result.at[index, :, 2 * c + k, pl.ds(FIRST, NX), :], there, o_send.at[index, 2 + k]).start()
+            pltpu.make_async_copy(result.at[index, part, 2 * c + k, pl.ds(FIRST, NX), :], there, o_send.at[index, 2 + k]).start()
 
     give(0)
     give(1)
@@ -493,8 +498,9 @@
             result[2, z, t, own, :] = sums[t] * (1.0 / 6.0) + c_buf[z + CHARGE, t, own, :]
         return 0
 
-    lax.fori_loop(0, OWN, last_sweep, 0, unroll=8)
-    give(2)
+    for first in (0, OWN // 2):
+        lax.fori_loop(first, first + OWN // 2, last_sweep, 0, unroll=4)
+        give(2, first, OWN // 2)
 
     exchange(c_buf, 0, CHARGE, ways, False)
     exchange(u2, 1, EARLY, ways, False)

time: 32.7 us -> 32.6 us (level)
  no operation moved by 1% of the time
where the time goes in v5:
time: 32.6 us; the launch traced here: 32.5 us
  Pallas kernels  31.9 us (98%)
  between operations  0.64 us (2%)
    pallas_call x1, Pallas kernels, on_device(): pl.pallas_call(lambda *refs: kernel(sizes, *refs), out_shape=[pltpu.VMEM(...  31 us
    pallas_call x1, Pallas kernels, on_device(): pl.pallas_call(hand_over, out_shape=shapes, in_specs=[pl.BlockSpec(memory...  0.9 us

profile of v5, /device:TPU:31, one launch (start us, length us, event | category | flops | bytes accessed | tf_op | source)
XLA Modules:
  0.0 32.5 jit_solution(2693089244795052061)
XLA Ops:
  0.6 31.0 %shard_map.103 = (f32[16,16,256]{2,1,0:T(8,128)S(1)}, f32[16,16,256]{2,1,0:T(8,128)S(1)}, f32[16,16,256]{2,1,0:T(8,128)S(1)}) custom-call(f32[16,16,256]{2,1,0:T(8,128)} %refs_0_.1, f32[16,16,256]{2,1,0:T(8,128)} %refs_1_.1, f32[16,16,256]{2,1,0:T(8,128)} %refs_2_.1, f32[16,16,256]{2,1,0:T(8,128)} %refs_3_.1, f32[16,16,256]{2,1,0:T(8,128)} %refs_4_.1, ...), custom_call_target="tpu_custom_call" | custom-call | tf_op jit(solution)/shard_map/pallas_call | solution.py:540
  31.6 0.9 %shard_map.104 = (f32[16,16,256]{2,1,0:T(8,128)}, f32[16,16,256]{2,1,0:T(8,128)}, f32[16,16,256]{2,1,0:T(8,128)}) custom-call(f32[16,16,256]{2,1,0:T(8,128)S(1)} %get-tuple-element.6.refs_0_, f32[16,16,256]{2,1,0:T(8,128)S(1)} %get-tuple-element.7.refs_1_, f32[16,16,256]{2,1,0:T(8,128)S(1)} %get-tuple-element.8.refs_2_), custom_call_target="tpu_custom_call" | custom-call | tf_op jit(solution)/shard_map/pallas_call | solution.py:570
